TPU v7x, 32 devices: a whole 2x2x4 slice. The times are simulated.
32 devices in a mesh: rotor: 4 (over y, core), blk: 8 (over z, x).
Axes of the slice: x: 2, y: 2, z: 4, core: 2. Of those that a mesh axis runs over, the one named last changes fastest.
Arguments:
- positions: float32 [3, 131072], P(None, ('rotor', 'blk')), may hold values from -6 to 6
- strengths: float32 [3, 131072], P(None, ('rotor', 'blk'))
- blade_of_block: int32 [1024], P(('rotor', 'blk')), may hold values from 0 to 29
- circulation: float32 [30], replicated, may hold values from 0.5 to 2
- tile_source_dev: int32 [8192, 1], P(('rotor', 'blk')), may hold values from 0 to 31; in each aligned block of 256 rows (0 to 255, 256 to 511, ...) at most 12 rows name the same one
- tile_source_blk: int32 [8192], P(('rotor', 'blk')), may hold values from 0 to 31
- tile_target: int32 [8192], P(('rotor', 'blk')), may hold values from 0 to 31
- tile_count: int32 [32], P(('rotor', 'blk')), may hold values from 128 to 256, as said below
Outputs:
- velocity: float32 [3, 131072], P(None, ('rotor', 'blk'))
- strength_rate: float32 [3, 131072], P(None, ('rotor', 'blk'))
Inputs may be any that keep to these rules, and one draw needn't show every extreme that they name: `tile_source_dev`: among the 256 slots of one device no device number appears more than 12 times, and one appears exactly 12 times. `tile_count`: some device has all 256 slots live.
All inputs are finite; a program needn't handle non-finite values.
Results may differ from a plain program's by a relative error of at most 0.0003.
Values sent between devices are 32-bit elements; how exact they have to be, the bound alone decides.
A program may use at most 128 MiB of HBM per device.

v0:
```python
import math

import jax
import jax.numpy as jnp
from jax import lax
from jax.sharding import PartitionSpec as P

inverse_four_pi = 1.0 / (4.0 * math.pi)
core_square = 1.0
diffusion_rate = 2.0
highest = lax.Precision.HIGHEST


def with_halo(cells, sides, width):
    for axis, dim in sides:
        count = lax.axis_size(axis)
        ends = count - 1
        head = lax.slice_in_dim(cells, 0, width, axis=dim)
        tail = lax.slice_in_dim(cells, cells.shape[dim] - width, cells.shape[dim], axis=dim)
        cells = jnp.concatenate(
            [
                lax.ppermute(tail, axis, [(i, (i + 1) % count) for i in range(ends)]),
                cells,
                lax.ppermute(head, axis, [((i + 1) % count, i) for i in range(ends)]),
            ],
            axis=dim,
        )
    return cells


def cross_rows(left, right):
    return jnp.stack(
        [
            left[1] * right[2] - left[2] * right[1],
            left[2] * right[0] - left[0] * right[2],
            left[0] * right[1] - left[1] * right[0],
        ]
    )


def contract(matrix, values):
    return jnp.einsum("ts,cs->ct", matrix, values, precision=highest)


def kernels(target_pos, source_pos):
    offset_vec = target_pos[:, :, None] - source_pos[:, None, :]
    distance_sq = jnp.sum(offset_vec * offset_vec, axis=0)
    inverse = 1.0 / (distance_sq + core_square)
    green_kernel = inverse_four_pi * inverse * jnp.sqrt(inverse)
    return (green_kernel, 3.0 * green_kernel * inverse, jnp.exp(-distance_sq / core_square))


def toward(target, source, green_kernel, hessian, smooth):
    target_pos, target_str = (target[:3], target[3:])
    source_pos, source_str = (source[:3], source[3:])
    spin_src = cross_rows(source_pos, source_str)
    green_str = contract(green_kernel, source_str)
    velocity = contract(green_kernel, spin_src) - cross_rows(target_pos, green_str)
    along_axis = jnp.sum(target_str * target_pos, axis=0)[:, None] - jnp.einsum(
        "ct,cs->ts", target_str, source_pos, precision=highest
    )
    lever_arm = hessian * along_axis
    stretch = (
        cross_rows(target_pos, contract(lever_arm, source_str))
        - contract(lever_arm, spin_src)
        - cross_rows(target_str, green_str)
    )
    diffusion = contract(smooth, source_str) - jnp.sum(smooth, axis=1)[None, :] * target_str
    return jnp.concatenate([velocity, stretch + diffusion_rate * diffusion], axis=0)


def near_block(target, sources, validity):
    green_kernel, hessian, smooth = kernels(target[:3], sources[:3])
    return toward(target, sources, green_kernel, hessian, smooth * validity[None, :])


def tile_pair(target, source):
    green_kernel, hessian, smooth = kernels(target[:3], source[:3])
    forward = toward(target, source, green_kernel, hessian, smooth)
    backward = toward(source, target, green_kernel.T, hessian.T, smooth.T)
    return (forward, backward)


def send_requests(request):
    return lax.all_to_all(request, ("rotor", "blk"), split_axis=0, concat_axis=0, tiled=True)


def send_blocks(outgoing):
    return lax.all_to_all(outgoing, ("rotor", "blk"), split_axis=0, concat_axis=0, tiled=True)


def send_results(results):
    return lax.all_to_all(results, ("rotor", "blk"), split_axis=0, concat_axis=0, tiled=True)


def local(
    positions,
    strengths,
    blade_of_block,
    circulation,
    tile_source_dev,
    tile_source_blk,
    tile_target,
    tile_count,
):
    local_blocks = blade_of_block.shape[0]
    width = positions.shape[1] // local_blocks
    n_rotor = lax.axis_size("rotor")
    n_blk = lax.axis_size("blk")
    devices = n_rotor * n_blk
    magnitude = (
        jnp.sqrt(jnp.sum(strengths * strengths, axis=0)).reshape(local_blocks, width).sum(axis=1)
    )
    member = (
        blade_of_block[:, None] == jnp.arange(circulation.shape[0], dtype=jnp.int32)[None, :]
    ).astype(jnp.float32)
    totals, counted = lax.psum(
        (jnp.sum(member * magnitude[:, None], axis=0), jnp.sum(member, axis=0) * width),
        ("rotor", "blk"),
    )
    factor = circulation / (totals / jnp.maximum(counted, 1.0) + 1e-06)
    block_factor = jnp.sum(member * factor[None, :], axis=1)
    scaled = strengths * jnp.repeat(block_factor, width)[None, :]
    state = jnp.concatenate([positions, scaled], axis=0)
    blocks = state.reshape(6, local_blocks, width).transpose(1, 0, 2)
    padded = with_halo(state, (("blk", 1),), width)
    place = lax.axis_index("blk")
    validity = jnp.concatenate(
        [
            jnp.full((width,), place > 0),
            jnp.ones((local_blocks * width,), bool),
            jnp.full((width,), place < n_blk - 1),
        ]
    ).astype(jnp.float32)

    def near_one(index):
        start = index * width
        sources = lax.dynamic_slice_in_dim(padded, start, 3 * width, 1)
        weights = lax.dynamic_slice_in_dim(validity, start, 3 * width, 0)
        return near_block(blocks[index], sources, weights)

    near_group = math.gcd(local_blocks, 16)
    near = lax.map(
        jax.vmap(near_one), jnp.arange(local_blocks, dtype=jnp.int32).reshape(-1, near_group)
    )
    near = near.reshape(local_blocks, 6, width)
    capacity = tile_target.shape[0]
    slot_count = max(2, (3 * capacity + 2 * devices - 1) // (2 * devices))
    source_dev = tile_source_dev[:, 0]
    positions_idx = jnp.arange(capacity, dtype=jnp.int32)
    live_tile = (positions_idx < tile_count[0]).astype(jnp.float32)
    same_peer = (source_dev[:, None] == source_dev[None, :]) & (
        positions_idx[:, None] > positions_idx[None, :]
    )
    rank_in_peer = jnp.sum(same_peer.astype(jnp.int32), axis=1)
    slot_index = source_dev * slot_count + rank_in_peer
    wanted = (
        slot_index[None, :] == jnp.arange(devices * slot_count, dtype=jnp.int32)[:, None]
    ).astype(jnp.int32)
    request = (jnp.sum(wanted * (tile_source_blk[None, :] + 1), axis=1) - 1).reshape(
        devices, slot_count
    )
    asked = send_requests(request)
    present = (asked >= 0).astype(jnp.float32)
    outgoing = blocks[jnp.clip(asked, 0, local_blocks - 1)] * present[:, :, None, None]
    incoming = send_blocks(outgoing)
    sources = incoming.reshape(devices * slot_count, 6, width)[slot_index]
    targets = blocks[tile_target]
    tile_batch = math.gcd(capacity, 64)
    groups = capacity // tile_batch

    def tile_group(pair):
        return jax.vmap(tile_pair)(pair[0], pair[1])

    target_out, source_out = lax.map(
        tile_group,
        (
            targets.reshape(groups, tile_batch, 6, width),
            sources.reshape(groups, tile_batch, 6, width),
        ),
    )
    target_out = target_out.reshape(capacity, 6, width) * live_tile[:, None, None]
    source_out = source_out.reshape(capacity, 6, width) * live_tile[:, None, None]
    target_hot = (
        tile_target[None, :] == jnp.arange(local_blocks, dtype=jnp.int32)[:, None]
    ).astype(jnp.float32)
    cross_target = jnp.einsum("nc,cxp->nxp", target_hot, target_out, precision=highest)
    back = jnp.einsum("fc,cxp->fxp", wanted.astype(jnp.float32), source_out, precision=highest)
    returned = send_results(back.reshape(devices, slot_count, 6, width))
    return_hot = (
        asked.reshape(-1)[None, :] == jnp.arange(local_blocks, dtype=jnp.int32)[:, None]
    ).astype(jnp.float32)
    cross_source = jnp.einsum(
        "nf,fxp->nxp",
        return_hot,
        returned.reshape(devices * slot_count, 6, width),
        precision=highest,
    )
    total = near + cross_target + cross_source
    flat_terms = total.transpose(1, 0, 2).reshape(6, local_blocks * width)
    return (flat_terms[:3], flat_terms[3:])


def solution(mesh):
    placed = (
        P(None, ("rotor", "blk")),
        P(None, ("rotor", "blk")),
        P(("rotor", "blk")),
        P(),
        P(("rotor", "blk"), None),
        P(("rotor", "blk")),
        P(("rotor", "blk")),
        P(("rotor", "blk")),
    )
    return jax.shard_map(
        local,
        mesh=mesh,
        in_specs=placed,
        out_specs=(P(None, ("rotor", "blk")), P(None, ("rotor", "blk"))),
        check_vma=False,
    )
```

profile of v0, /device:TPU:0, one launch (start us, length us, event | category | flops | bytes accessed | tf_op | source)
XLA Modules:
  0.0 721.0 jit_solution(6770685092090512786)
XLA Ops:
  3.7 7.3 %all-to-all-start = ((s32[32,1,12]{2,1,0:T(1,128)}), s32[32,1,12]{2,1,0:T(1,128)S(1)}, u32[]{:S(2)}, u32[]{:S(2)}) async-start(s32[32,1,12]{2,1,0:T(1,128)} %bitcast.65), calls=%async_computation | async-start | bytes 32768 | tf_op jit(solution)/shard_map/all_to_all | solution.py:85
  12.7 40.5 %all-reduce.2 = (f32[30]{0:T(128)S(1)}, f32[30]{0:T(128)S(1)}) all-reduce(f32[30]{0:T(128)S(1)} %get-tuple-element.104, f32[30]{0:T(128)S(1)} %broadcast_multiply_fusion.4), channel_id=1, replica_groups=mesh['rotor'=4,'blk'=8] {'rotor','blk'}, use_global_device_ids=true, to_apply=%region_3.0 | all-reduce | flops 60 | bytes 480 | tf_op jit(solution)/shard_map/psum | solution.py:117
  79.8 25.1 %all-to-all-done.1 = f32[32,12,6,128]{3,2,1,0:T(8,128)S(1)} async-done(((f32[32,12,6,128]{3,2,1,0:T(8,128)}), f32[32,12,6,128]{3,2,1,0:T(8,128)S(1)}, u32[]{:S(2)}, u32[]{:S(2)}) %all-to-all-start.1) | async-done | bytes 1179680 | tf_op jit(solution)/shard_map/all_to_all | solution.py:89
  107.1 416.8 %while.29 = (s32[]{:T(128)}, f32[4,64,6,128]{3,1,0,2:T(8,128)}, f32[4,64,6,128]{3,1,0,2:T(8,128)}, f32[4,64,6,128]{3,1,2,0:T(8,128)}, f32[4,64,6,128]{3,1,2,0:T(8,128)S(1)}, /*index=5*/s32[]{:T(128)}) while((s32[]{:T(128)}, f32[4,64,6,128]{3,1,0,2:T(8,128)}, f32[4,64,6,128]{3,1,0,2:T(8,128)}, f32[4,64,6,128]{3,1,2,0:T(8,128)}, ...), condition=%wide.region_20.21_spmd, body=%wide.region_14.20_spmd.sunk | while | flops 495419392 | bytes 144605344 | solution.py:175
  116.2 6.6 fusion.211
  122.8 8.4 %fusion.214 = f32[64,128,128]{1,2,0:T(8,128)S(1)} fusion(f32[64,128]{1,0:T(8,128)S(1)} %get-tuple-element.490, f32[64,3,128]{2,0,1:T(8,128)S(1)} %get-tuple-element.473, f32[64,3,128]{2,0,1:T(8,128)S(1)} %get-tuple-element.469, f32[64,128,128]{2,1,0:T(8,128)S(1)} %multiply_reduce_fusion.13), kind=kOutput, calls=%fused_computation.10.clone.1 | convolution fusion | flops 46137344 | bytes 8617984 | tf_op jit(solution)/shard_map/while/body/eval_jaxpr/vmap(ct,cs->ts)/dot_general | solution.py:59
  142.0 5.6 copy.502
  147.6 9.2 %fusion.224 = f32[64,3,128]{2,1,0:T(4,128)S(1)} fusion(f32[64,128,128]{1,2,0:T(8,128)} %copy.502, f32[3,64,128]{2,1,0:T(8,128)S(1)} %pad_maximum_fusion.18), kind=kOutput, calls=%fused_computation.21.clone.1 | convolution fusion | flops 39845888 | bytes 4390912 | tf_op jit(solution)/shard_map/while/body/eval_jaxpr/vmap(ts,cs->ct)/dot_general | solution.py:42
  156.8 7.2 fusion.212
  168.7 4.7 fusion.219
  176.8 5.6 copy.503
  182.4 10.4 %subtract_multiply_fusion.5 = f32[64,128,128]{2,1,0:T(8,128)S(1)} fusion(f32[64,128,128]{2,1,0:T(8,128)} %copy.503, f32[64,128]{1,0:T(8,128)S(1)} %get-tuple-element.471, f32[64,3,128]{2,0,1:T(8,128)S(1)} %get-tuple-element.472, f32[64,3,128]{2,0,1:T(8,128)S(1)} %get-tuple-element.468, f32[64,128,128]{2,1,0:T(8,128)} %copy-done.1), kind=kOutput, calls=%fused_computation.12.clone.1 | convolution fusion | flops 42991616 | bytes 12812288 | tf_op jit(solution)/shard_map/while/body/eval_jaxpr/vmap(ct,cs->ts)/dot_general | solution.py:59
  192.9 6.6 fusion.217
  199.4 6.6 fusion.207
  216.1 6.6 fusion.211
  222.7 8.4 %fusion.214 = f32[64,128,128]{1,2,0:T(8,128)S(1)} fusion(f32[64,128]{1,0:T(8,128)S(1)} %get-tuple-element.490, f32[64,3,128]{2,0,1:T(8,128)S(1)} %get-tuple-element.473, f32[64,3,128]{2,0,1:T(8,128)S(1)} %get-tuple-element.469, f32[64,128,128]{2,1,0:T(8,128)S(1)} %multiply_reduce_fusion.13), kind=kOutput, calls=%fused_computation.10.clone.1 | convolution fusion | flops 46137344 | bytes 8617984 | tf_op jit(solution)/shard_map/while/body/eval_jaxpr/vmap(ct,cs->ts)/dot_general | solution.py:59
  241.9 5.6 copy.502
  247.5 9.2 %fusion.224 = f32[64,3,128]{2,1,0:T(4,128)S(1)} fusion(f32[64,128,128]{1,2,0:T(8,128)} %copy.502, f32[3,64,128]{2,1,0:T(8,128)S(1)} %pad_maximum_fusion.18), kind=kOutput, calls=%fused_computation.21.clone.1 | convolution fusion | flops 39845888 | bytes 4390912 | tf_op jit(solution)/shard_map/while/body/eval_jaxpr/vmap(ts,cs->ct)/dot_general | solution.py:42
  256.7 7.2 fusion.212
  276.7 5.6 copy.503
  282.3 10.4 %subtract_multiply_fusion.5 = f32[64,128,128]{2,1,0:T(8,128)S(1)} fusion(f32[64,128,128]{2,1,0:T(8,128)} %copy.503, f32[64,128]{1,0:T(8,128)S(1)} %get-tuple-element.471, f32[64,3,128]{2,0,1:T(8,128)S(1)} %get-tuple-element.472, f32[64,3,128]{2,0,1:T(8,128)S(1)} %get-tuple-element.468, f32[64,128,128]{2,1,0:T(8,128)} %copy-done.1), kind=kOutput, calls=%fused_computation.12.clone.1 | convolution fusion | flops 42991616 | bytes 12812288 | tf_op jit(solution)/shard_map/while/body/eval_jaxpr/vmap(ct,cs->ts)/dot_general | solution.py:59
  292.7 6.6 fusion.217
  299.3 6.6 fusion.207
  315.9 6.6 fusion.211
  322.5 8.4 %fusion.214 = f32[64,128,128]{1,2,0:T(8,128)S(1)} fusion(f32[64,128]{1,0:T(8,128)S(1)} %get-tuple-element.490, f32[64,3,128]{2,0,1:T(8,128)S(1)} %get-tuple-element.473, f32[64,3,128]{2,0,1:T(8,128)S(1)} %get-tuple-element.469, f32[64,128,128]{2,1,0:T(8,128)S(1)} %multiply_reduce_fusion.13), kind=kOutput, calls=%fused_computation.10.clone.1 | convolution fusion | flops 46137344 | bytes 8617984 | tf_op jit(solution)/shard_map/while/body/eval_jaxpr/vmap(ct,cs->ts)/dot_general | solution.py:59
  341.7 5.6 copy.502
  347.3 9.2 %fusion.224 = f32[64,3,128]{2,1,0:T(4,128)S(1)} fusion(f32[64,128,128]{1,2,0:T(8,128)} %copy.502, f32[3,64,128]{2,1,0:T(8,128)S(1)} %pad_maximum_fusion.18), kind=kOutput, calls=%fused_computation.21.clone.1 | convolution fusion | flops 39845888 | bytes 4390912 | tf_op jit(solution)/shard_map/while/body/eval_jaxpr/vmap(ts,cs->ct)/dot_general | solution.py:42
  356.5 7.2 fusion.212
  376.5 5.6 copy.503
  382.2 10.4 %subtract_multiply_fusion.5 = f32[64,128,128]{2,1,0:T(8,128)S(1)} fusion(f32[64,128,128]{2,1,0:T(8,128)} %copy.503, f32[64,128]{1,0:T(8,128)S(1)} %get-tuple-element.471, f32[64,3,128]{2,0,1:T(8,128)S(1)} %get-tuple-element.472, f32[64,3,128]{2,0,1:T(8,128)S(1)} %get-tuple-element.468, f32[64,128,128]{2,1,0:T(8,128)} %copy-done.1), kind=kOutput, calls=%fused_computation.12.clone.1 | convolution fusion | flops 42991616 | bytes 12812288 | tf_op jit(solution)/shard_map/while/body/eval_jaxpr/vmap(ct,cs->ts)/dot_general | solution.py:59
  392.6 6.6 fusion.217
  399.2 6.6 fusion.207
  415.8 6.6 fusion.211
  422.4 8.4 %fusion.214 = f32[64,128,128]{1,2,0:T(8,128)S(1)} fusion(f32[64,128]{1,0:T(8,128)S(1)} %get-tuple-element.490, f32[64,3,128]{2,0,1:T(8,128)S(1)} %get-tuple-element.473, f32[64,3,128]{2,0,1:T(8,128)S(1)} %get-tuple-element.469, f32[64,128,128]{2,1,0:T(8,128)S(1)} %multiply_reduce_fusion.13), kind=kOutput, calls=%fused_computation.10.clone.1 | convolution fusion | flops 46137344 | bytes 8617984 | tf_op jit(solution)/shard_map/while/body/eval_jaxpr/vmap(ct,cs->ts)/dot_general | solution.py:59
  441.6 5.6 copy.502
  447.2 9.2 %fusion.224 = f32[64,3,128]{2,1,0:T(4,128)S(1)} fusion(f32[64,128,128]{1,2,0:T(8,128)} %copy.502, f32[3,64,128]{2,1,0:T(8,128)S(1)} %pad_maximum_fusion.18), kind=kOutput, calls=%fused_computation.21.clone.1 | convolution fusion | flops 39845888 | bytes 4390912 | tf_op jit(solution)/shard_map/while/body/eval_jaxpr/vmap(ts,cs->ct)/dot_general | solution.py:42
  456.4 7.2 fusion.212
  476.4 5.6 copy.503
  482.0 10.4 %subtract_multiply_fusion.5 = f32[64,128,128]{2,1,0:T(8,128)S(1)} fusion(f32[64,128,128]{2,1,0:T(8,128)} %copy.503, f32[64,128]{1,0:T(8,128)S(1)} %get-tuple-element.471, f32[64,3,128]{2,0,1:T(8,128)S(1)} %get-tuple-element.472, f32[64,3,128]{2,0,1:T(8,128)S(1)} %get-tuple-element.468, f32[64,128,128]{2,1,0:T(8,128)} %copy-done.1), kind=kOutput, calls=%fused_computation.12.clone.1 | convolution fusion | flops 42991616 | bytes 12812288 | tf_op jit(solution)/shard_map/while/body/eval_jaxpr/vmap(ct,cs->ts)/dot_general | solution.py:59
  492.5 6.6 fusion.217
  499.0 6.6 fusion.207
  531.9 186.4 %while.28 = (s32[]{:T(128)}, f32[2,16,6,128]{3,1,0,2:T(8,128)S(1)}, s32[2,16]{1,0:T(2,128)S(1)}, f32[6,4352]{1,0:T(8,128)}, f32[32,6,128]{2,1,0:T(8,128)S(1)}, /...) while((s32[]{:T(128)}, f32[2,16,6,128]{3,1,0,2:T(8,128)S(1)}, ...), condition=%wide.region_11.12_spmd, body=%wide.region_7.11_spmd.sunk | while | flops 192960656 | bytes 30571508 | solution.py:143
  531.9 32.7 %while.31 = (s32[]{:T(128)}, f32[4352]{0:T(1024)}, s32[16,1]{0,1:T(1,128)S(1)}, f32[16,384]{1,0:T(8,128)S(1)}, s32[]{:T(128)}, /*index=5*/s32[]{:T(128)}) while((s32[]{:T(128)}, f32[4352]{0:T(1024)}, s32[16,1]{0,1:T(1,128)S(1)}, f32[16,384]{1,0:T(8,128)S(1)}, s32[]{:T(128)}, /*index=5*/s32[]{:T(128)}) %tuple.176), condition=%wide.while_cond.1, body=%wide.while_body.1.sunk | while | flops 2 | bytes 9313 | solution.py:139
  565.3 32.7 %while.30 = (s32[]{:T(128)}, f32[6,4352]{1,0:T(8,128)}, s32[16,2]{0,1:T(2,128)S(1)}, f32[16,6,384]{2,1,0:T(8,128)S(1)}, s32[]{:T(128)}) while((s32[]{:T(128)}, f32[6,4352]{1,0:T(8,128)}, s32[16,2]{0,1:T(2,128)S(1)}, f32[16,6,384]{2,1,0:T(8,128)S(1)}, s32[]{:T(128)}) %tuple.173), condition=%wide.while_cond, body=%wide.while_body.sunk | while | flops 2 | bytes 21609 | solution.py:138
  604.8 5.2 subtract_multiply_fusion.4
  625.1 32.7 %while.31 = (s32[]{:T(128)}, f32[4352]{0:T(1024)}, s32[16,1]{0,1:T(1,128)S(1)}, f32[16,384]{1,0:T(8,128)S(1)}, s32[]{:T(128)}, /*index=5*/s32[]{:T(128)}) while((s32[]{:T(128)}, f32[4352]{0:T(1024)}, s32[16,1]{0,1:T(1,128)S(1)}, f32[16,384]{1,0:T(8,128)S(1)}, s32[]{:T(128)}, /*index=5*/s32[]{:T(128)}) %tuple.176), condition=%wide.while_cond.1, body=%wide.while_body.1.sunk | while | flops 2 | bytes 9313 | solution.py:139
  658.5 32.7 %while.30 = (s32[]{:T(128)}, f32[6,4352]{1,0:T(8,128)}, s32[16,2]{0,1:T(2,128)S(1)}, f32[16,6,384]{2,1,0:T(8,128)S(1)}, s32[]{:T(128)}) while((s32[]{:T(128)}, f32[6,4352]{1,0:T(8,128)}, s32[16,2]{0,1:T(2,128)S(1)}, f32[16,6,384]{2,1,0:T(8,128)S(1)}, s32[]{:T(128)}) %tuple.173), condition=%wide.while_cond, body=%wide.while_body.sunk | while | flops 2 | bytes 21609 | solution.py:138
  698.0 5.2 subtract_multiply_fusion.4
  (494 shorter events, 346.2 us)
Async XLA Ops:
  2.3 0.5 copy-start.10
  3.7 53.0 %all-to-all-start = ((s32[32,1,12]{2,1,0:T(1,128)}), s32[32,1,12]{2,1,0:T(1,128)S(1)}, u32[]{:S(2)}, u32[]{:S(2)}) async-start(s32[32,1,12]{2,1,0:T(1,128)} %bitcast.65), calls=%async_computation | async-start | bytes 32768 | tf_op jit(solution)/shard_map/all_to_all | solution.py:85
  55.7 10.3 %copy-start.4 = (f32[3,4096]{1,0:T(4,128)}, f32[3,4096]{1,0:T(4,128)S(1)}, u32[]{:S(2)}) copy-start(f32[3,4096]{1,0:T(4,128)S(1)} %broadcast_multiply_fusion.3) | copy-start | bytes 147460
  56.6 19.8 %copy-start.2 = (f32[32,6,128]{2,1,0:T(8,128)}, f32[32,6,128]{2,1,0:T(8,128)S(1)}, u32[]{:S(2)}) copy-start(f32[32,6,128]{2,1,0:T(8,128)S(1)} %fusion.88) | copy-start | bytes 294916
  58.0 8.1 %copy-start.6 = (f32[3,4096]{1,0:T(4,128)S(1)}, f32[3,4096]{1,0:T(4,128)}, u32[]{:S(2)}) copy-start(f32[3,4096]{1,0:T(4,128)} %param.12) | copy-start | bytes 147460
  58.0 16.0 %copy-start.15 = (s32[256]{0:T(256)S(1)}, s32[256]{0:T(256)}, u32[]{:S(2)}) copy-start(s32[256]{0:T(256)} %param.18) | copy-start | bytes 3076
  58.0 16.0 %copy-start.9 = (s32[256,1]{0,1:T(1,128)S(1)}, s32[256,1]{0,1:T(1,128)}, u32[]{:S(2)}) copy-start(s32[256,1]{0,1:T(1,128)} %param.16) | copy-start | bytes 3076
  61.6 43.3 %all-to-all-start.1 = ((f32[32,12,6,128]{3,2,1,0:T(8,128)}), f32[32,12,6,128]{3,2,1,0:T(8,128)S(1)}, u32[]{:S(2)}, u32[]{:S(2)}) async-start(f32[32,12,6,128]{3,2,1,0:T(8,128)} %broadcast_multiply_fusion.1), calls=%async_computation.1 | async-start | bytes 3145728 | tf_op jit(solution)/shard_map/all_to_all | solution.py:89
  66.7 11.6 %collective-permute-start = (f32[6,128]{1,0:T(8,128)}, f32[6,128]{1,0:T(8,128)}, u32[]{:S(2)}, u32[]{:S(2)}) collective-permute-start(f32[6,128]{1,0:T(8,128)} %get-tuple-element.226), channel_id=1, source_target_pairs={{0,1},{1,2},{2,3},{3,4},{4,5},{5,6},{6,7},{8,9},{9,10},{10,11},{11... | collective-permute-start | bytes 9224 | tf_op jit(solution)/shard_map/ppermute | solution.py:22
  70.9 7.3 %collective-permute-start.1 = (f32[6,128]{1,0:T(8,128)}, f32[6,128]{1,0:T(8,128)}, u32[]{:S(2)}, u32[]{:S(2)}) collective-permute-start(f32[6,128]{1,0:T(8,128)} %get-tuple-element.227), channel_id=1, source_target_pairs={{1,0},{2,1},{3,2},{4,3},{5,4},{6,5},{7,6},{9,8},{10,9},{11,10},{12... | collective-permute-start | bytes 9224 | tf_op jit(solution)/shard_map/ppermute | solution.py:24
  107.1 416.9 %copy-start.13 = (f32[4,64]{1,0:T(4,128)S(1)}, f32[4,64]{1,0:T(4,128)}, u32[]{:S(2)}) copy-start(f32[4,64]{1,0:T(4,128)} %fusion.97) | copy-start | bytes 3076
  107.1 418.2 %copy-start.8 = (s32[32,12]{0,1:T(8,128)S(1)}, s32[32,12]{0,1:T(8,128)}, u32[]{:S(2)}) copy-start(s32[32,12]{0,1:T(8,128)} %multiply_add_fusion) | copy-start | bytes 4612
  107.1 418.2 %copy-start.11 = (s32[256]{0:T(256)S(1)}, s32[256]{0:T(256)}, u32[]{:S(2)}) copy-start(s32[256]{0:T(256)} %copy-done.10) | copy-start | bytes 3076
  112.7 26.1 %copy-start.1 = (f32[64,128,128]{2,1,0:T(8,128)}, f32[64,128,128]{2,1,0:T(8,128)S(1)}, u32[]{:S(2)}) copy-start(f32[64,128,128]{2,1,0:T(8,128)S(1)} %multiply_reduce_fusion.13) | copy-start | bytes 12582916 | tf_op jit(solution)/shard_map/while
  147.6 9.2 %copy-start = (f32[64,128,128]{1,2,0:T(8,128)S(1)}, f32[64,128,128]{1,2,0:T(8,128)}, u32[]{:S(2)}) copy-start(f32[64,128,128]{1,2,0:T(8,128)} %copy.502) | copy-start | bytes 12582916 | tf_op jit(solution)/shard_map/while
  212.5 26.1 %copy-start.1 = (f32[64,128,128]{2,1,0:T(8,128)}, f32[64,128,128]{2,1,0:T(8,128)S(1)}, u32[]{:S(2)}) copy-start(f32[64,128,128]{2,1,0:T(8,128)S(1)} %multiply_reduce_fusion.13) | copy-start | bytes 12582916 | tf_op jit(solution)/shard_map/while
  247.5 9.2 %copy-start = (f32[64,128,128]{1,2,0:T(8,128)S(1)}, f32[64,128,128]{1,2,0:T(8,128)}, u32[]{:S(2)}) copy-start(f32[64,128,128]{1,2,0:T(8,128)} %copy.502) | copy-start | bytes 12582916 | tf_op jit(solution)/shard_map/while
  312.4 26.1 %copy-start.1 = (f32[64,128,128]{2,1,0:T(8,128)}, f32[64,128,128]{2,1,0:T(8,128)S(1)}, u32[]{:S(2)}) copy-start(f32[64,128,128]{2,1,0:T(8,128)S(1)} %multiply_reduce_fusion.13) | copy-start | bytes 12582916 | tf_op jit(solution)/shard_map/while
  347.3 9.2 %copy-start = (f32[64,128,128]{1,2,0:T(8,128)S(1)}, f32[64,128,128]{1,2,0:T(8,128)}, u32[]{:S(2)}) copy-start(f32[64,128,128]{1,2,0:T(8,128)} %copy.502) | copy-start | bytes 12582916 | tf_op jit(solution)/shard_map/while
  412.2 26.1 %copy-start.1 = (f32[64,128,128]{2,1,0:T(8,128)}, f32[64,128,128]{2,1,0:T(8,128)S(1)}, u32[]{:S(2)}) copy-start(f32[64,128,128]{2,1,0:T(8,128)S(1)} %multiply_reduce_fusion.13) | copy-start | bytes 12582916 | tf_op jit(solution)/shard_map/while
  447.2 9.2 %copy-start = (f32[64,128,128]{1,2,0:T(8,128)S(1)}, f32[64,128,128]{1,2,0:T(8,128)}, u32[]{:S(2)}) copy-start(f32[64,128,128]{1,2,0:T(8,128)} %copy.502) | copy-start | bytes 12582916 | tf_op jit(solution)/shard_map/while
  525.3 6.5 copy-start.3
  525.3 6.5 copy-start.7
  525.3 6.5 copy-start.14
  528.4 190.5 %all-to-all-start.2 = ((f32[32,12,6,128]{3,2,1,0:T(8,128)}), f32[32,12,6,128]{3,2,1,0:T(8,128)S(1)}, u32[]{:S(2)}, u32[]{:S(2)}) async-start(f32[32,12,6,128]{3,2,1,0:T(8,128)} %copy.348), calls=%async_computation.2 | async-start | bytes 3145728 | tf_op jit(solution)/shard_map/all_to_all | solution.py:93
  531.8 186.4 %copy-start.5 = (f32[4,64,6,128]{3,1,0,2:T(8,128)S(1)}, f32[4,64,6,128]{3,1,0,2:T(8,128)}, u32[]{:S(2)}) copy-start(f32[4,64,6,128]{3,1,0,2:T(8,128)} %get-tuple-element.63) | copy-start | bytes 2359300
  531.8 186.4 %copy-start.17 = (f32[256]{0:T(256)S(1)}, f32[256]{0:T(256)}, u32[]{:S(2)}) copy-start(f32[256]{0:T(256)} %compare_convert_fusion.1) | copy-start | bytes 3076
  531.9 186.5 %copy-start.16 = (s32[256]{0:T(256)S(1)}, s32[256]{0:T(256)}, u32[]{:S(2)}) copy-start(s32[256]{0:T(256)} %param.18) | copy-start | bytes 3076
  531.9 187.0 %copy-start.12 = (s32[384]{0:T(512)S(1)}, s32[384]{0:T(512)}, u32[]{:S(2)}) copy-start(s32[384]{0:T(512)} %eq.96) | copy-start | bytes 4612
where the time goes:
time: 731 us; the launch traced here: 721 us
  matrix products  352 us (48%)
  local copies, waits for them, and re-layouts  193 us (26%)
  other arithmetic  67.8 us (9%)
  blocking collectives  40.5 us (6%)
  waiting for transfers between devices  25.1 us (3%)
  starting transfers between devices  20.7 us (3%)
  loops' own time  19.9 us (3%)
    dot_general x50, matrix products, contract(): return jnp.einsum('ts,cs->ct', matrix, values, precision=highest)  264 us
    gather x224, local copies, waits for them, and re-layouts  130 us
    dot_general x10, matrix products, toward(): jnp.einsum('ct,cs->ts', target_str, source_pos, precision=highest)  85.9 us
    psum x1, blocking collectives, local(): lax.psum((jnp.sum(member * magnitude[:, None], axis=0), jnp.sum(member, a...  40.5 us
    all_to_all x1, waiting for transfers between devices, send_blocks(): lax.all_to_all(outgoing, ('rotor', 'blk'), split_axis=0, concat_axis=0, t...  25.1 us
    mul x4, local copies, waits for them, and re-layouts, kernels(): 3.0 * green_kernel * inverse  22.5 us
    div x4, local copies, waits for them, and re-layouts, kernels(): inverse = 1.0 / (distance_sq + core_square)  22.4 us
    reduce_sum x6, other arithmetic, kernels(): distance_sq = jnp.sum(offset_vec * offset_vec, axis=0)  19.6 us
  transfers between devices with their start and end apart: 5, of which 1 were waited for; matrix products, arithmetic and copies ran while one was open for 28% of the time, Pallas kernels for 0%

commit v1 on v0

v1 whole, which is shorter than its diff:
```python
import functools
import math

import jax
import jax.numpy as jnp
from jax import lax
from jax.experimental import pallas as pl
from jax.experimental.pallas import tpu as pltpu
from jax.sharding import PartitionSpec as P

AXES = ("rotor", "blk")
green_scale = 1.0 / (4.0 * math.pi)
smooth_scale = 2.0 * math.e
log2_e = math.log2(math.e)
ROWS = 8
f32, bf16 = jnp.float32, jnp.bfloat16


def split3(v):
    hi = v.astype(bf16)
    rest = v - hi.astype(f32)
    mid = rest.astype(bf16)
    return hi, mid, (rest - mid.astype(f32)).astype(bf16)


def split2(v):
    hi = v.astype(bf16)
    return hi, (v - hi.astype(f32)).astype(bf16)


def roll(v, up):
    return pltpu.roll(v, (ROWS - up) % ROWS, 0)


def row_ids(width):
    return lax.broadcasted_iota(jnp.int32, (ROWS, width), 0)


def features(raw, factor):
    row = row_ids(raw.shape[1])
    is_str = ((row >= 3) & (row < 6)) | (row == 7)
    base = jnp.where(is_str, raw * factor, raw)
    xx = jnp.where(row < 3, base, roll(base, 5))
    aa = jnp.where(row < 3, roll(base, 3), base)
    x1, x2, a1, a2 = roll(xx, 1), roll(xx, 2), roll(aa, 1), roll(aa, 2)
    spin = jnp.where(row < 3, x1 * a2 - x2 * a1, 0.0)
    group = jnp.where(row < 5, aa, jnp.where(row == 5, 1.0, 0.0))
    hi, lo = split2(jnp.concatenate([group, spin], axis=0))
    values = jnp.concatenate([hi, lo], axis=0)
    return base, values, (x1, x2, a1, a2, aa)


def source_front(base):
    row = row_ids(base.shape[1])
    full = jnp.concatenate([base, jnp.where(row == 0, 1.0, 0.0)], axis=0)
    hi, mid, lo = split3(full)
    return jnp.concatenate([hi, hi, mid, mid, hi, lo], axis=0)


def target_front(base):
    row = row_ids(base.shape[1])
    norm, along = base[6:7], base[7:8]
    zero = jnp.zeros_like(base)
    dist = jnp.concatenate(
        [
            jnp.where(row < 3, -2.0 * base, jnp.where(row == 6, 1.0, 0.0)),
            jnp.where(row == 0, norm + 1.0, zero),
        ],
        axis=0,
    )
    to_target = jnp.concatenate(
        [jnp.where(row < 3, -roll(base, 3), 0.0), jnp.where(row == 0, along, zero)], axis=0
    )
    shifted = roll(base, 5)
    to_source = jnp.concatenate(
        [
            jnp.where((row >= 3) & (row < 6), -shifted, jnp.where(row == 7, 1.0, 0.0)),
            zero,
        ],
        axis=0,
    )
    hi, mid, lo = split3(jnp.concatenate([dist, to_target, to_source], axis=1))
    return jnp.concatenate([hi, mid, hi, mid, lo, hi], axis=0)


def combine(sums, own):
    width = sums.shape[1] // 3
    x1, x2, a1, a2, aa = own
    half = sums.shape[0] // 2
    sums = sums[:half] + sums[half:]
    ga, la, ea = (sums[:ROWS, i * width : (i + 1) * width] for i in range(3))
    gs, ls = (sums[ROWS:, i * width : (i + 1) * width] for i in range(2))
    ga1, ga2, la1, la2 = roll(ga, 1), roll(ga, 2), roll(la, 1), roll(la, 2)
    u = green_scale * (gs - (x1 * ga2 - x2 * ga1))
    w = (
        (3.0 * green_scale) * (x1 * la2 - x2 * la1 - ls)
        - green_scale * (a1 * ga2 - a2 * ga1)
        + smooth_scale * (ea - ea[5:6] * aa)
    )
    return jnp.where(row_ids(width) < 4, u, roll(w, 4))


def pair(front_s, values_s, own_s, front_t, values_t, own_t, both):
    width = values_s.shape[1]
    d = lax.dot_general(
        front_s, front_t, (((0,), (0,)), ((), ())), preferred_element_type=f32
    )
    p = d[:, :width]
    inv = lax.rsqrt(p)
    inv2 = inv * inv
    g = inv2 * inv
    h = g * inv2
    e = jnp.exp2(p * (-log2_e))
    g2, e2 = split2(g), split2(e)
    l2 = split2(h * d[:, width : 2 * width])
    ahead = jnp.concatenate(
        [jnp.concatenate([g2[i], l2[i], e2[i]], axis=1) for i in range(2)], axis=0
    )
    lhs = jnp.concatenate([values_s, values_s], axis=1)
    to_t = combine(jnp.dot(lhs, ahead, preferred_element_type=f32), own_t)
    if not both:
        return to_t, None
    m2 = split2(h * d[:, 2 * width :])
    back = jnp.concatenate(
        [jnp.concatenate([v[0], v[1]], axis=1) for v in (g2, m2, e2)], axis=0
    )
    lhs = jnp.concatenate([values_t, values_t], axis=1)
    sums = lax.dot_general(lhs, back, (((1,), (1,)), ((), ())), preferred_element_type=f32)
    return to_t, combine(sums, own_s)


def prepare(state, factor_of, front, values, own, sources=None):
    def step(k, carry):
        base, vals, perm = features(state[k], factor_of(k))
        front[k] = target_front(base)
        values[k] = vals
        for i, v in enumerate(perm):
            own[k, i] = v
        if sources is not None:
            sources[k] = source_front(base)
        return carry

    lax.fori_loop(0, state.shape[0], step, 0)


def near_kernel(factor, state, out, front, values, own, sources):
    prepare(state, lambda k: factor[k], front, values, own, sources)
    blocks = state.shape[0]

    def held(k):
        return values[k], tuple(own[k, i] for i in range(5))

    def alone(k, carry):
        v, o = held(k)
        out[k] = pair(sources[k], v, o, front[k], v, o, False)[0]
        return carry

    lax.fori_loop(0, blocks, alone, 0)

    def chain(k, carry):
        vs, os = held(k + 1)
        vt, ot = held(k)
        to_t, to_s = pair(sources[k + 1], vs, os, front[k], vt, ot, True)
        out[k] += to_t
        out[k + 1] += to_s
        return carry

    lax.fori_loop(0, blocks - 1, chain, 0)


def tile_kernel(live, target, source, factor, first, state, near, acc, dense, front, values, own):
    mine = acc.shape[0]
    prepare(near.at[1], lambda k: factor[first[0] + k], front, values, own)

    def clear(k, carry):
        dense[pl.ds(k * 16, 16)] = jnp.zeros((16,) + dense.shape[1:], f32)
        return carry

    lax.fori_loop(0, dense.shape[0] // 16, clear, 0)

    def start(k, carry):
        acc[k] = near[0, k]
        return carry

    lax.fori_loop(0, mine, start, 0)

    def one(c):
        t, s = target[c], source[c]
        base, vs, os = features(state[s], factor[s])
        vt, ot = values[t], tuple(own[t, i] for i in range(5))
        return t, s, pair(source_front(base), vs, os, front[t], vt, ot, True)

    def add(t, s, terms):
        acc[t] += terms[0]
        dense[s] += terms[1]

    count = live[0]

    def step(c, carry):
        add(*one(c))
        return carry

    def two(c, carry):
        first_one, second_one = one(2 * c), one(2 * c + 1)
        add(*first_one)
        add(*second_one)
        return carry

    lax.fori_loop(0, count // 2, two, 0)
    lax.fori_loop(count // 2 * 2, count, step, 0)


def scratch(blocks, width):
    return [
        pltpu.VMEM((blocks, 96, 3 * width), bf16),
        pltpu.VMEM((blocks, 32, width), bf16),
        pltpu.VMEM((blocks, 5, ROWS, width), f32),
    ]


smem = pl.BlockSpec(memory_space=pltpu.SMEM)
vmem = pl.BlockSpec(memory_space=pltpu.VMEM)


def near_field(factor, state):
    blocks, _, width = state.shape
    return pl.pallas_call(
        near_kernel,
        out_shape=jax.ShapeDtypeStruct(state.shape, f32),
        in_specs=[smem, vmem],
        out_specs=vmem,
        scratch_shapes=scratch(blocks, width) + [pltpu.VMEM((blocks, 96, width), bf16)],
        compiler_params=pltpu.CompilerParams(vmem_limit_bytes=24 * 2**20),
        cost_estimate=pl.CostEstimate(
            flops=blocks * width * width * 400, bytes_accessed=2**20, transcendentals=0
        ),
    )(factor, state)


def tiles(live, target, source, factor, first, state, near):
    blocks, width = near.shape[1], near.shape[3]
    return pl.pallas_call(
        tile_kernel,
        out_shape=(
            jax.ShapeDtypeStruct(near.shape[1:], f32),
            jax.ShapeDtypeStruct(state.shape, f32),
        ),
        in_specs=[smem] * 5 + [vmem] * 2,
        out_specs=(vmem, vmem),
        scratch_shapes=scratch(blocks, width),
        compiler_params=pltpu.CompilerParams(vmem_limit_bytes=48 * 2**20),
    )(live, target, source, factor, first, state, near)


def local(
    positions,
    strengths,
    blade_of_block,
    circulation,
    tile_source_dev,
    tile_source_blk,
    tile_target,
    tile_count,
):
    blocks = blade_of_block.shape[0]
    width = positions.shape[1] // blocks
    n_blk = lax.axis_size("blk")
    place = lax.axis_index("blk")
    me = lax.axis_index("rotor") * n_blk + place

    magnitude = jnp.sqrt(jnp.sum(strengths * strengths, axis=0)).reshape(blocks, width).sum(axis=1)
    facts = jnp.concatenate([magnitude, blade_of_block.astype(f32)]).reshape(1, -1)
    state = jnp.concatenate(
        [
            positions,
            strengths,
            jnp.sum(positions * positions, axis=0, keepdims=True),
            jnp.sum(positions * strengths, axis=0, keepdims=True),
        ],
        axis=0,
    )
    state = state.reshape(ROWS, blocks, width).transpose(1, 0, 2)
    every_fact = lax.all_gather(facts, AXES, axis=0, tiled=True)
    everyone = lax.all_gather(state, AXES, axis=0, tiled=True)

    member = (
        every_fact[:, blocks:].reshape(-1, 1)
        == jnp.arange(circulation.shape[0], dtype=jnp.int32).astype(f32)[None, :]
    ).astype(f32)
    totals = jnp.sum(member * every_fact[:, :blocks].reshape(-1, 1), axis=0)
    counted = jnp.sum(member, axis=0) * width
    blade_factor = circulation / (totals / jnp.maximum(counted, 1.0) + 1e-06)
    factor = jnp.sum(member * blade_factor[None, :], axis=1)
    own_factor = lax.dynamic_slice_in_dim(factor, me * blocks, blocks)
    near = near_field(own_factor, state)

    has_next = (place < n_blk - 1).astype(jnp.int32)
    source = tile_source_dev[:, 0] * blocks + tile_source_blk
    total = lax.axis_size("rotor") * n_blk * blocks
    edge_source = jnp.minimum((me + 1) * blocks, total - 1)
    target = jnp.concatenate([tile_target, jnp.zeros((1,), jnp.int32)])
    source = jnp.concatenate([source, jnp.zeros((1,), jnp.int32)])
    target = jnp.where(
        jnp.arange(target.shape[0]) == tile_count[0], blocks - 1, target
    ).astype(jnp.int32)
    source = jnp.where(
        jnp.arange(source.shape[0]) == tile_count[0], edge_source, source
    ).astype(jnp.int32)
    live = tile_count + has_next
    first = (me * blocks).astype(jnp.int32).reshape(1)
    acc, dense = tiles(live, target, source, factor, first, everyone, jnp.stack([near, state]))
    returned = lax.psum_scatter(dense, AXES, scatter_dimension=0, tiled=True)
    out = (acc + returned).transpose(1, 0, 2).reshape(ROWS, blocks * width)
    return out[:3], out[4:7]


def solution(mesh):
    placed = (
        P(None, AXES),
        P(None, AXES),
        P(AXES),
        P(),
        P(AXES, None),
        P(AXES),
        P(AXES),
        P(AXES),
    )
    return jax.shard_map(
        local,
        mesh=mesh,
        in_specs=placed,
        out_specs=(P(None, AXES), P(None, AXES)),
        check_vma=False,
    )
```

time: 731 us -> 329 us (0.45); the launches traced: 721 us -> 329 us
  matrix products: 352 us -> 0 us
  local copies, waits for them, and re-layouts: 193 us -> 3.93 us
  waiting for transfers between devices: 25.1 us -> 157 us
  Pallas kernels: 0 us -> 104 us
  other arithmetic: 67.8 us -> 7.51 us
  starting transfers between devices: 20.7 us -> 0.08 us
  loops' own time: 19.9 us -> 0 us
  between operations: 1.89 us -> 14.8 us
    dot_general x63 -> x0, matrix products: 352 us -> none  [the longest x50 264 us: contract(): return jnp.einsum('ts,cs->ct', matrix, values, precision=highest)]
    reduce_scatter x0 -> x1, waiting for transfers between devices: none -> 157 us  [local(): returned = lax.psum_scatter(dense, AXES, scatter_dimension=0, tiled=True)]
    gather x229 -> x0, local copies, waits for them, and re-layouts: 135 us -> none
    pallas_call x0 -> x2, Pallas kernels: none -> 104 us  [the longest x1 78.2 us: tiles(): pl.pallas_call(tile_kernel, out_shape=(jax.ShapeDtypeStruct(near.shape[1:...]
    unnamed x0 -> x1, blocking collectives: none -> 42.1 us
    psum x1 -> x0, blocking collectives: 40.5 us -> none  [local(): lax.psum((jnp.sum(member * magnitude[:, None], axis=0), jnp.sum(member, a...]
    reduce_sum x24 -> x4, other arithmetic: 37.5 us -> 1.41 us  [the longest x1 1 us: local(): jnp.sum(positions * positions, axis=0, keepdims=True)]
    all_to_all x3 -> x0, waiting for transfers between devices: 25.1 us -> none  [the longest x1 25.1 us: send_blocks(): lax.all_to_all(outgoing, ('rotor', 'blk'), split_axis=0, concat_axis=0, t...]
  transfers between devices with their start and end apart: 5 -> 2, of which waited for: 1 -> 1; matrix products, arithmetic and copies ran while one was open for 28% -> 1% of each run, Pallas kernels for 0% -> 8%
where the time goes in v1:
time: 329 us
  waiting for transfers between devices  157 us (48%)
  Pallas kernels  104 us (32%)
  blocking collectives  42.1 us (13%)
  between operations  14.8 us (4%)
  other arithmetic  7.51 us (2%)
  local copies, waits for them, and re-layouts  3.93 us (1%)
    reduce_scatter x1, waiting for transfers between devices, local(): returned = lax.psum_scatter(dense, AXES, scatter_dimension=0, tiled=True)  157 us
    pallas_call x1, Pallas kernels, tiles(): pl.pallas_call(tile_kernel, out_shape=(jax.ShapeDtypeStruct(near.shape[1:...  78.2 us
    unnamed x1, blocking collectives  42.1 us
    pallas_call x1, Pallas kernels, near_field(): pl.pallas_call(near_kernel, out_shape=jax.ShapeDtypeStruct(state.shape, f...  25.9 us
  transfers between devices with their start and end apart: 2, of which 1 were waited for; matrix products, arithmetic and copies ran while one was open for 1% of the time, Pallas kernels for 8%

profile of v1, /device:TPU:0, one launch (start us, length us, event | category | flops | bytes accessed | tf_op | source)
XLA Modules:
  0.0 329.4 jit_solution(15759838061983244404)
XLA Ops:
  7.2 0.0 all-gather.3.cloned.1.call-start
  7.2 1.0 multiply_reduce_fusion.1
  8.2 1.6 fusion.3
  9.8 0.0 all-gather.3.cloned.1.call-update
  9.8 0.0 reduce-scatter.2.cloned.1.call-start
  10.5 0.7 convert_element_type.14
  11.2 0.1 bitcast_reduce_fusion
  11.3 0.2 maximum_dynamic-update-slice_fusion
  11.5 42.1 %all-reduce = f32[2048]{0:T(1024)S(1)} all-reduce(f32[2048]{0:T(1024)S(1)} %maximum_dynamic-update-slice_fusion), channel_id=2, replica_groups=mesh['rotor'=4,'blk'=8] {'rotor','blk'}, use_global_device_ids=true, to_apply=%add | all-reduce | flops 2048 | bytes 16384
  53.6 0.1 reshape.37
  53.7 0.1 fusion.7
  53.7 0.1 mul.55
  53.8 0.1 eq.25
  53.9 0.7 broadcast_multiply_fusion
  54.6 0.7 add.34
  55.3 0.2 fusion.1
  55.5 0.7 add_divide_fusion
  56.1 0.1 fusion.2.factor
  56.2 0.1 dynamic_slice.3.factor
  56.3 0.0 copy-start.1
  56.3 1.0 copy-done.1
  57.3 25.9 %shard_map.95 = f32[32,8,128]{2,1,0:T(8,128)S(1)} custom-call(f32[32]{0:T(128)S(1)} %dynamic_slice.3.factor, f32[32,8,128]{2,1,0:T(8,128)S(1)} %copy-done.1), custom_call_target="tpu_custom_call" | custom-call | flops 209715200 | bytes 1048576 | tf_op jit(solution)/shard_map/pallas_call | solution.py:227
  83.2 0.7 fusion.5
  84.0 0.0 all-gather.3.cloned.1.call-done.state
  84.0 78.2 %shard_map.96 = (f32[32,8,128]{2,1,0:T(8,128)S(1)}, f32[1024,8,128]{2,1,0:T(8,128)S(1)}) custom-call(s32[1]{0:T(128)S(6)} %add.31.live, s32[257]{0:T(512)S(1)} %get-tuple-element.17.target, s32[257]{0:T(512)S(1)} %get-tuple-element.18.source, f32[1024]{0:T(1024)S(1)} %fusion.2.factor, s32[1]{0:T(128)} %bitcast.4.first, ...), custom_call_target="tpu_custom_call" | custom-call | tf_op jit(solution)/shard_map/pallas_call | solution.py:242
  162.2 0.0 copy-start
  162.2 1.9 copy-done
  164.1 0.0 reduce-scatter.2.cloned.1.call-update
  164.1 156.8 %reduce-scatter.2.cloned.1.call-done = f32[32,8,128]{2,1,0:T(8,128)} async-done(((f32[1024,8,128]{2,1,0:T(8,128)}), f32[32,8,128]{2,1,0:T(8,128)}) %reduce-scatter.2.cloned.1.call-update) | async-done | bytes 131088 | tf_op jit(solution)/shard_map/reduce_scatter | solution.py:312
  320.9 0.9 add_bitcast_fusion
  321.9 0.7 slice_bitcast_fusion
  (3 shorter events, 0.0 us)
Async XLA Ops:
  7.2 76.8 %all-gather.3.cloned.1.call-start = ((), (), s32[]{:S(2)}) async-start(), calls=%async_computation.1 | async-start | bytes 4325376 | tf_op jit(solution)/shard_map/all_gather | solution.py:284
  9.8 311.1 %reduce-scatter.2.cloned.1.call-start = ((), (), s32[]{:S(2)}) async-start(), calls=%async_computation.2 | async-start | bytes 4325376 | tf_op jit(solution)/shard_map/reduce_scatter | solution.py:312
  56.3 1.0 copy-start.1
  162.2 1.9 copy-start
Sparse Core Ops, SparseCore 0:
  11.0 64.7 all-gather.2
  164.2 156.6 reduce-scatter.1

commit v2 on v1

v2 whole, which is shorter than its diff:
```python
import functools
import math

import jax
import jax.numpy as jnp
from jax import lax
from jax.experimental import pallas as pl
from jax.experimental.pallas import tpu as pltpu
from jax.sharding import PartitionSpec as P

AXES = ("rotor", "blk")
green_scale = 1.0 / (4.0 * math.pi)
smooth_scale = 2.0 * math.e
log2_e = math.log2(math.e)
ROWS = 8
f32, bf16 = jnp.float32, jnp.bfloat16


def split3(v):
    hi = v.astype(bf16)
    rest = v - hi.astype(f32)
    mid = rest.astype(bf16)
    return hi, mid, (rest - mid.astype(f32)).astype(bf16)


def split2(v):
    hi = v.astype(bf16)
    return hi, (v - hi.astype(f32)).astype(bf16)


def roll(v, up):
    return pltpu.roll(v, (ROWS - up) % ROWS, 0)


def row_ids(width):
    return lax.broadcasted_iota(jnp.int32, (ROWS, width), 0)


def features(raw, factor):
    row = row_ids(raw.shape[1])
    base = jnp.where(row >= 3, raw * factor, raw)
    xx = jnp.where(row < 3, base, roll(base, 5))
    aa = jnp.where(row < 3, roll(base, 3), base)
    norm = jnp.sum(jnp.where(row < 3, base * base, 0.0), axis=0, keepdims=True)
    along = jnp.sum(jnp.where(row < 3, base * aa, 0.0), axis=0, keepdims=True)
    base = jnp.where(row == 6, norm, jnp.where(row == 7, along, base))
    x1, x2, a1, a2 = roll(xx, 1), roll(xx, 2), roll(aa, 1), roll(aa, 2)
    spin = jnp.where(row < 3, x1 * a2 - x2 * a1, 0.0)
    group = jnp.where(row < 5, aa, jnp.where(row == 5, 1.0, 0.0))
    hi, lo = split2(jnp.concatenate([group, spin], axis=0))
    values = jnp.concatenate([hi, lo], axis=0)
    return base, values, (x1, x2, a1, a2, aa)


def source_front(base):
    row = row_ids(base.shape[1])
    full = jnp.concatenate([base, jnp.where(row == 0, 1.0, 0.0)], axis=0)
    hi, mid, lo = split3(full)
    return jnp.concatenate([hi, hi, mid, mid, hi, lo], axis=0)


def target_front(base):
    row = row_ids(base.shape[1])
    norm, along = base[6:7], base[7:8]
    zero = jnp.zeros_like(base)
    dist = jnp.concatenate(
        [
            jnp.where(row < 3, -2.0 * base, jnp.where(row == 6, 1.0, 0.0)),
            jnp.where(row == 0, norm + 1.0, zero),
        ],
        axis=0,
    )
    to_target = jnp.concatenate(
        [jnp.where(row < 3, -roll(base, 3), 0.0), jnp.where(row == 0, along, zero)], axis=0
    )
    shifted = roll(base, 5)
    to_source = jnp.concatenate(
        [
            jnp.where((row >= 3) & (row < 6), -shifted, jnp.where(row == 7, 1.0, 0.0)),
            zero,
        ],
        axis=0,
    )
    hi, mid, lo = split3(jnp.concatenate([dist, to_target, to_source], axis=1))
    return jnp.concatenate([hi, mid, hi, mid, lo, hi], axis=0)


def combine(sums, own):
    width = sums.shape[1] // 3
    x1, x2, a1, a2, aa = own
    half = sums.shape[0] // 2
    sums = sums[:half] + sums[half:]
    ga, la, ea = (sums[:ROWS, i * width : (i + 1) * width] for i in range(3))
    gs, ls = (sums[ROWS:, i * width : (i + 1) * width] for i in range(2))
    ga1, ga2, la1, la2 = roll(ga, 1), roll(ga, 2), roll(la, 1), roll(la, 2)
    u = green_scale * (gs - (x1 * ga2 - x2 * ga1))
    w = (
        (3.0 * green_scale) * (x1 * la2 - x2 * la1 - ls)
        - green_scale * (a1 * ga2 - a2 * ga1)
        + smooth_scale * (ea - ea[5:6] * aa)
    )
    return jnp.where(row_ids(width) < 4, u, roll(w, 4))


def pair(front_s, values_s, own_s, front_t, values_t, own_t, both):
    width = values_s.shape[1]
    d = lax.dot_general(
        front_s, front_t, (((0,), (0,)), ((), ())), preferred_element_type=f32
    )
    p = d[:, :width]
    inv = lax.rsqrt(p)
    inv2 = inv * inv
    g = inv2 * inv
    h = g * inv2
    e = jnp.exp2(p * (-log2_e))
    g2, e2 = split2(g), split2(e)
    l2 = split2(h * d[:, width : 2 * width])
    ahead = jnp.concatenate(
        [jnp.concatenate([g2[i], l2[i], e2[i]], axis=1) for i in range(2)], axis=0
    )
    lhs = jnp.concatenate([values_s, values_s], axis=1)
    to_t = combine(jnp.dot(lhs, ahead, preferred_element_type=f32), own_t)
    if not both:
        return to_t, None
    m2 = split2(h * d[:, 2 * width :])
    back = jnp.concatenate(
        [jnp.concatenate([v[0], v[1]], axis=1) for v in (g2, m2, e2)], axis=0
    )
    lhs = jnp.concatenate([values_t, values_t], axis=1)
    sums = lax.dot_general(lhs, back, (((1,), (1,)), ((), ())), preferred_element_type=f32)
    return to_t, combine(sums, own_s)


def exchange_kernel(rows, out, landing, send, receive):
    n = rows.shape[0]
    n_blk = lax.axis_size("blk")
    me = lax.axis_index("rotor") * n_blk + lax.axis_index("blk")

    def where(peer):
        return (peer // n_blk, lax.rem(peer, n_blk))

    barrier = pltpu.get_barrier_semaphore()

    def greet(d, carry):
        pl.semaphore_signal(
            barrier,
            inc=1,
            device_id=where(lax.rem(me + d, n)),
            device_id_type=pl.DeviceIdType.MESH,
        )
        return carry

    lax.fori_loop(1, n, greet, 0)
    pl.semaphore_wait(barrier, n - 1)

    def copy(d):
        peer = lax.rem(me + d, n)
        return pltpu.make_async_remote_copy(
            src_ref=rows.at[peer],
            dst_ref=landing.at[me],
            send_sem=send.at[d],
            recv_sem=receive.at[d],
            device_id=where(peer),
            device_id_type=pl.DeviceIdType.MESH,
        )

    def start(d, carry):
        copy(d).start()
        return carry

    lax.fori_loop(1, n, start, 0)
    landing[me] = rows[me]

    def finish(d, carry):
        copy(d).wait()
        return carry

    lax.fori_loop(1, n, finish, 0)
    out[...] = landing[...]


def gather_kernel(asked, state, out):
    def step(p, carry):
        block = state[jnp.maximum(asked[p], 0)]
        out[pl.ds(p * 6, 6)] = block[:6]
        return carry

    lax.fori_loop(0, asked.shape[0], step, 0)


def prepare(state, factor_of, front, values, own, sources=None):
    def step(k, carry):
        base, vals, perm = features(state[k], factor_of(k))
        front[k] = target_front(base)
        values[k] = vals
        for i, v in enumerate(perm):
            own[k, i] = v
        if sources is not None:
            sources[k] = source_front(base)
        return carry

    lax.fori_loop(0, state.shape[0], step, 0)


def near_kernel(factor, ends, state, out, total, front, values, own, sources):
    prepare(state, lambda k: factor[k], front, values, own, sources)
    blocks = out.shape[0]

    def held(k):
        return values[k], tuple(own[k, i] for i in range(5))

    def chain(k):
        vs, os = held(k + 1)
        vt, ot = held(k)
        return pair(sources[k + 1], vs, os, front[k], vt, ot, True)

    def alone(k):
        v, o = held(k)
        return pair(sources[k], v, o, front[k], v, o, False)[0]

    total[1] = chain(0)[1] * ends[0]

    def both(k, carry):
        itself = alone(k)
        to_t, to_s = chain(k)
        total[k] += itself + to_t
        total[k + 1] = to_s
        return carry

    lax.fori_loop(1, blocks, both, 0)
    total[blocks] += alone(blocks) + chain(blocks)[0] * ends[1]
    out[...] = total[1 : blocks + 1]


def tile_kernel(
    part, live, target, place, share, origin, factor, first, state, arrived, before, acc, back,
    front, values, own, chosen,
):
    mine = acc.shape[0]
    prepare(state, lambda k: factor[first[0] + k], front, values, own)
    acc[...] = before[...]

    def choose(c, held):
        chosen[held] = c
        return held + (share[c] == part).astype(jnp.int32)

    count = lax.fori_loop(0, live[0], choose, jnp.int32(0))
    width = acc.shape[2]

    def one(i):
        c = chosen[i]
        t, p = target[c], place[c]
        raw = arrived[pl.ds(p * 6, 6)]
        raw = jnp.concatenate([raw, jnp.zeros((2, width), f32)], axis=0)
        base, vs, os = features(raw, factor[origin[c]])
        vt, ot = values[t], tuple(own[t, i] for i in range(5))
        return t, p, pair(source_front(base), vs, os, front[t], vt, ot, True)

    def add(t, p, terms):
        acc[t] += terms[0]
        back[pl.ds(p * 6, 6)] = jnp.concatenate([terms[1][:3], terms[1][4:7]], axis=0)

    def step(i, carry):
        add(*one(i))
        return carry

    def two(i, carry):
        first_one, second_one = one(2 * i), one(2 * i + 1)
        add(*first_one)
        add(*second_one)
        return carry

    lax.fori_loop(0, count // 2, two, 0)
    lax.fori_loop(count // 2 * 2, count, step, 0)


def final_kernel(*refs):
    asked, near, acc = refs[:3]
    returned, (velocity, rate, total) = refs[3:-3], refs[-3:]
    blocks, _, width = near.shape
    total[pl.ds(0, blocks)] = near[...] + acc[...]
    slots = asked.shape[0] // len(returned)
    for i, got in enumerate(returned):

        def step(p, carry):
            index = asked[i * slots + p]
            index = jnp.where(index < 0, blocks, index)
            terms = got[pl.ds(p * 6, 6)]
            gap = jnp.zeros((1, width), f32)
            total[index] += jnp.concatenate([terms[:3], gap, terms[3:], gap], axis=0)
            return carry

        lax.fori_loop(0, slots, step, 0)
    for k in range(blocks):
        velocity[:, k * width : (k + 1) * width] = total[k][:3]
        rate[:, k * width : (k + 1) * width] = total[k][4:7]


def scratch(blocks, width):
    return [
        pltpu.VMEM((blocks, 96, 3 * width), bf16),
        pltpu.VMEM((blocks, 32, width), bf16),
        pltpu.VMEM((blocks, 5, ROWS, width), f32),
    ]


smem = pl.BlockSpec(memory_space=pltpu.SMEM)
vmem = pl.BlockSpec(memory_space=pltpu.VMEM)
params = pltpu.CompilerParams(vmem_limit_bytes=24 * 2**20)


def exchange(rows):
    n = rows.shape[0]
    return pl.pallas_call(
        exchange_kernel,
        out_shape=jax.ShapeDtypeStruct(rows.shape, f32),
        in_specs=[vmem],
        out_specs=vmem,
        scratch_shapes=[
            pltpu.VMEM(rows.shape, f32),
            pltpu.SemaphoreType.DMA((n,)),
            pltpu.SemaphoreType.DMA((n,)),
        ],
        compiler_params=pltpu.CompilerParams(collective_id=0, has_side_effects=True),
    )(rows)


def gather(asked, state):
    return pl.pallas_call(
        gather_kernel,
        out_shape=jax.ShapeDtypeStruct((asked.shape[0] * 6, state.shape[2]), f32),
        in_specs=[smem, vmem],
        out_specs=vmem,
        compiler_params=params,
    )(asked, state)


def near_field(factor, ends, state):
    padded, _, width = state.shape
    return pl.pallas_call(
        near_kernel,
        out_shape=jax.ShapeDtypeStruct((padded - 2, ROWS, width), f32),
        in_specs=[smem, smem, vmem],
        out_specs=vmem,
        scratch_shapes=[pltpu.VMEM((padded, ROWS, width), f32)]
        + scratch(padded, width)
        + [pltpu.VMEM((padded, 96, width), bf16)],
        compiler_params=params,
        cost_estimate=pl.CostEstimate(
            flops=20 * 10**9, bytes_accessed=2**20, transcendentals=0
        ),
    )(factor, ends, state)


def tiles(part, scalars, state, arrived, before):
    blocks, _, width = state.shape
    return pl.pallas_call(
        functools.partial(tile_kernel, part),
        out_shape=(
            jax.ShapeDtypeStruct(state.shape, f32),
            jax.ShapeDtypeStruct(arrived.shape, f32),
        ),
        in_specs=[smem] * len(scalars) + [vmem] * 3,
        out_specs=(vmem, vmem),
        scratch_shapes=scratch(blocks, width)
        + [pltpu.SMEM((scalars[1].shape[0] + 1,), jnp.int32)],
        compiler_params=params,
        cost_estimate=pl.CostEstimate(
            flops=30 * 10**9, bytes_accessed=2**20, transcendentals=0
        ),
    )(*scalars, state, arrived, before)


def finish(asked, near, acc, returned):
    blocks, _, width = near.shape
    shape = jax.ShapeDtypeStruct((3, blocks * width), f32)
    return pl.pallas_call(
        final_kernel,
        out_shape=(shape, shape),
        in_specs=[smem] + [vmem] * (2 + len(returned)),
        out_specs=(vmem, vmem),
        scratch_shapes=[pltpu.VMEM((blocks + 1, ROWS, width), f32)],
        compiler_params=params,
    )(asked, near, acc, *returned)


PARTS = 2


def local(
    positions,
    strengths,
    blade_of_block,
    circulation,
    tile_source_dev,
    tile_source_blk,
    tile_target,
    tile_count,
):
    blocks = blade_of_block.shape[0]
    width = positions.shape[1] // blocks
    n_blk = lax.axis_size("blk")
    devices = lax.axis_size("rotor") * n_blk
    place = lax.axis_index("blk")
    me = lax.axis_index("rotor") * n_blk + place
    capacity = tile_target.shape[0]
    slot_count = max(2, (3 * capacity + 2 * devices - 1) // (2 * devices))
    each = -(-slot_count // PARTS)

    source_dev = tile_source_dev[:, 0]
    ids = jnp.arange(capacity, dtype=jnp.int32)
    earlier = (source_dev[:, None] == source_dev[None, :]) & (ids[:, None] > ids[None, :])
    rank = jnp.sum(earlier.astype(jnp.int32), axis=1)
    share = rank // each
    spot = source_dev * each + rank % each
    origin = source_dev * blocks + tile_source_blk
    ask = jnp.where(ids < tile_count[0], tile_source_blk, -1)
    peer_hot = source_dev[None, :] == jnp.arange(devices, dtype=jnp.int32)[:, None]
    rank_hot = rank[None, :] == jnp.arange(PARTS * each, dtype=jnp.int32)[:, None]
    request = (
        jnp.sum(
            jnp.where(
                peer_hot[:, None, :] & rank_hot[None, :, :], (ask + 1)[None, None, :], 0
            ),
            axis=2,
        )
        - 1
    )

    magnitude = jnp.sqrt(jnp.sum(strengths * strengths, axis=0)).reshape(blocks, width).sum(axis=1)
    facts = jnp.concatenate([magnitude, blade_of_block.astype(f32)])
    rows = jnp.concatenate(
        [
            request.astype(f32),
            jnp.broadcast_to(facts[None, :], (devices, 2 * blocks)),
        ],
        axis=1,
    )
    used = PARTS * each
    rows = jnp.pad(rows, ((0, 0), (0, -rows.shape[1] % 128)))
    got = exchange(rows[:, None, :])[:, 0]
    asked = got[:, :used].astype(jnp.int32)
    asked = asked.reshape(devices, PARTS, each).transpose(1, 0, 2)
    member = (
        got[:, used + blocks : used + 2 * blocks].reshape(-1, 1)
        == jnp.arange(circulation.shape[0], dtype=jnp.int32).astype(f32)[None, :]
    ).astype(f32)
    totals = jnp.sum(member * got[:, used : used + blocks].reshape(-1, 1), axis=0)
    counted = jnp.sum(member, axis=0) * width
    blade_factor = circulation / (totals / jnp.maximum(counted, 1.0) + 1e-06)
    factor = jnp.sum(member * blade_factor[None, :], axis=1)

    state = jnp.concatenate(
        [positions, strengths, jnp.zeros((2, positions.shape[1]), f32)], axis=0
    )
    state = state.reshape(ROWS, blocks, width).transpose(1, 0, 2)

    def swap(flat):
        return lax.all_to_all(flat, AXES, split_axis=0, concat_axis=0, tiled=True)

    up = [(i, i + 1) for i in range(n_blk - 1)]
    down = [(i + 1, i) for i in range(n_blk - 1)]
    padded = jnp.concatenate(
        [
            lax.ppermute(state[blocks - 1 :], "blk", up),
            state,
            lax.ppermute(state[:1], "blk", down),
        ],
        axis=0,
    )
    state, padded = lax.optimization_barrier((state, padded))
    arrived = [swap(gather(asked[i].reshape(-1), state)) for i in range(PARTS)]
    ends = jnp.stack([place > 0, place < n_blk - 1]).astype(f32)
    around = jnp.concatenate([jnp.zeros((1,), f32), factor, jnp.zeros((1,), f32)])
    near_factor = lax.dynamic_slice_in_dim(around, me * blocks, blocks + 2)
    first = (me * blocks).astype(jnp.int32).reshape(1)
    scalars = (tile_count, tile_target, spot, share, origin, factor, first)
    acc = jnp.zeros((blocks, ROWS, width), f32)
    returned = []
    for i in range(PARTS):
        acc, back = tiles(i, scalars, state, arrived[i], acc)
        returned.append(swap(back))
    padded, acc = lax.optimization_barrier((padded, acc))
    near = near_field(near_factor, ends, padded)
    return finish(asked.reshape(-1), near, acc, returned)


def solution(mesh):
    placed = (
        P(None, AXES),
        P(None, AXES),
        P(AXES),
        P(),
        P(AXES, None),
        P(AXES),
        P(AXES),
        P(AXES),
    )
    return jax.shard_map(
        local,
        mesh=mesh,
        in_specs=placed,
        out_specs=(P(None, AXES), P(None, AXES)),
        check_vma=False,
    )
```

time: 329 us -> 187 us (0.57)
  waiting for transfers between devices: 157 us -> 24.1 us
  starting transfers between devices: 0.08 us -> 50.9 us
  blocking collectives: 42.1 us -> 0 us
  between operations: 14.8 us -> 1.58 us
  Pallas kernels: 104 us -> 97.7 us
  local copies, waits for them, and re-layouts: 3.93 us -> 8.81 us
  other arithmetic: 7.51 us -> 2.86 us
    reduce_scatter x1 -> x0, waiting for transfers between devices: 157 us -> none  [local(): returned = lax.psum_scatter(dense, AXES, scatter_dimension=0, tiled=True)]
    all_to_all x0 -> x4, starting transfers between devices: none -> 44.1 us  [swap(): return lax.all_to_all(flat, AXES, split_axis=0, concat_axis=0, tiled=True)]
    unnamed x1 -> x0, blocking collectives: 42.1 us -> none
    all_to_all x0 -> x4, waiting for transfers between devices: none -> 24.1 us  [swap(): return lax.all_to_all(flat, AXES, split_axis=0, concat_axis=0, tiled=True)]
    ppermute x0 -> x2, starting transfers between devices: none -> 6.76 us  [the longest x1 5.47 us: local(): lax.ppermute(state[blocks - 1:], 'blk', up)]
    pallas_call x2 -> x7, Pallas kernels: 104 us -> 97.7 us  [the longest x2 57.6 us: tiles(): pl.pallas_call(functools.partial(tile_kernel, part), out_shape=(jax.Shape...]
    all_to_all x0 -> x8, local copies, waits for them, and re-layouts: none -> 3.69 us  [swap(): return lax.all_to_all(flat, AXES, split_axis=0, concat_axis=0, tiled=True)]
  transfers between devices with their start and end apart: 2 -> 6, of which waited for: 1 -> 2; matrix products, arithmetic and copies ran while one was open for 1% -> 2% of each run, Pallas kernels for 8% -> 49%
where the time goes in v2:
time: 187 us; the launch traced here: 186 us
  Pallas kernels  97.7 us (52%)
  starting transfers between devices  50.9 us (27%)
  waiting for transfers between devices  24.1 us (13%)
  local copies, waits for them, and re-layouts  8.81 us (5%)
  other arithmetic  2.86 us (2%)
    pallas_call x2, Pallas kernels, tiles(): pl.pallas_call(functools.partial(tile_kernel, part), out_shape=(jax.Shape...  57.6 us
    all_to_all x4, starting transfers between devices, swap(): return lax.all_to_all(flat, AXES, split_axis=0, concat_axis=0, tiled=True)  44.1 us
    all_to_all x4, waiting for transfers between devices, swap(): return lax.all_to_all(flat, AXES, split_axis=0, concat_axis=0, tiled=True)  24.1 us
    pallas_call x1, Pallas kernels, near_field(): pl.pallas_call(near_kernel, out_shape=jax.ShapeDtypeStruct((padded - 2, R...  21.2 us
    pallas_call x1, Pallas kernels, exchange(): pl.pallas_call(exchange_kernel, out_shape=jax.ShapeDtypeStruct(rows.shape...  10.9 us
    ppermute x1, starting transfers between devices, local(): lax.ppermute(state[blocks - 1:], 'blk', up)  5.47 us
    pallas_call x1, Pallas kernels, finish(): pl.pallas_call(final_kernel, out_shape=(shape, shape), in_specs=[smem] +...  4.37 us
  transfers between devices with their start and end apart: 6, of which 2 were waited for; matrix products, arithmetic and copies ran while one was open for 2% of the time, Pallas kernels for 49%

profile of v2, /device:TPU:0, one launch (start us, length us, event | category | flops | bytes accessed | tf_op | source)
XLA Modules:
  0.0 186.0 jit_solution(15164705345187148190)
XLA Ops:
  0.6 0.1 pad.10.clone
  0.7 1.0 maximum_bitcast_fusion.state
  1.7 1.3 collective-permute-start.1
  3.0 5.5 %collective-permute-start = (f32[1,8,128]{2,1,0:T(8,128)S(1)}, f32[1,8,128]{2,1,0:T(8,128)S(1)}, u32[]{:S(2)}, u32[]{:S(2)}) collective-permute-start(f32[1,8,128]{2,1,0:T(8,128)S(1)} %get-tuple-element.20), channel_id=1, source_target_pairs={{0,1},{1,2},{2,3},{3,4},{4,5},{5,6},{6,7},{8,9},{9,10},{10,11},{11... | collective-permute-start | bytes 12296 | tf_op jit(solution)/shard_map/ppermute | solution.py:465
  8.5 0.2 convert_reduce_fusion
  9.5 0.7 copy-done.4
  10.1 0.3 select_reduce_fusion
  10.4 0.1 copy.19
  10.5 0.6 copy-done.6
  11.2 0.1 bitcast_reduce_fusion
  11.3 0.1 pad_maximum_fusion.2
  11.4 0.6 pad.4
  12.0 10.9 %shard_map.95 = f32[32,1,128]{2,1,0:T(1,128)} custom-call(f32[32,1,128]{2,1,0:T(1,128)} %bitcast.21), custom_call_target="tpu_custom_call" | custom-call | tf_op jit(solution)/shard_map/pallas_call | solution.py:314
  22.9 0.7 slice_convert_fusion
  23.7 0.1 copy.21
  23.8 0.1 copy.24
  23.9 0.1 reshape_squeeze.7.asked
  24.0 1.9 %shard_map.97 = f32[1152,128]{1,0:T(8,128)S(1)} custom-call(s32[192]{0:T(256)S(1)} %reshape_squeeze.7.asked, f32[32,8,128]{2,1,0:T(8,128)S(1)} %maximum_bitcast_fusion.state), custom_call_target="tpu_custom_call" | custom-call | tf_op jit(solution)/shard_map/pallas_call | solution.py:329
  25.9 0.9 all_to_all.31
  26.8 4.5 %all-to-all-start.1 = ((f32[32,36,128]{2,1,0:T(8,128)}), f32[32,36,128]{2,1,0:T(8,128)S(1)}, u32[]{:S(2)}, u32[]{:S(2)}) async-start(f32[32,36,128]{2,1,0:T(8,128)} %all_to_all.31), calls=%async_computation.1 | async-start | bytes 1310720 | tf_op jit(solution)/shard_map/all_to_all | solution.py:459
  31.2 0.1 copy.22
  31.3 0.1 reshape.80.refs_0_
  31.5 0.6 copy-done.1
  32.1 0.1 fusion.7
  32.1 0.1 eq.76
  32.2 0.1 mul.44
  32.3 0.1 copy.23
  32.4 0.1 reshape_squeeze.6.asked
  32.5 0.2 fusion.2
  32.7 0.7 copy-done.5
  33.4 0.1 fusion.3.factor
  33.5 0.1 concatenate.17
  33.5 0.1 dynamic_slice.3.factor
  33.6 0.1 add_convert_fusion.1.ends
  33.7 1.9 %shard_map.96 = f32[1152,128]{1,0:T(8,128)S(1)} custom-call(s32[192]{0:T(256)S(1)} %reshape_squeeze.6.asked, f32[32,8,128]{2,1,0:T(8,128)S(1)} %maximum_bitcast_fusion.state), custom_call_target="tpu_custom_call" | custom-call | tf_op jit(solution)/shard_map/pallas_call | solution.py:329
  35.6 0.9 all_to_all.28
  36.4 14.0 %all-to-all-done.1 = f32[32,36,128]{2,1,0:T(8,128)S(1)} async-done(((f32[32,36,128]{2,1,0:T(8,128)}), f32[32,36,128]{2,1,0:T(8,128)S(1)}, u32[]{:S(2)}, u32[]{:S(2)}) %all-to-all-start.1) | async-done | bytes 589856 | tf_op jit(solution)/shard_map/all_to_all | solution.py:459
  50.4 2.6 %all-to-all-start = ((f32[32,36,128]{2,1,0:T(8,128)}), f32[32,36,128]{2,1,0:T(8,128)S(1)}, u32[]{:S(2)}, u32[]{:S(2)}) async-start(f32[32,36,128]{2,1,0:T(8,128)} %all_to_all.28), calls=%async_computation | async-start | bytes 1310720 | tf_op jit(solution)/shard_map/all_to_all | solution.py:459
  53.1 0.7 copy-done
  53.8 49.5 %shard_map.98 = (f32[32,8,128]{2,1,0:T(8,128)S(1)}, f32[1152,128]{1,0:T(8,128)S(1)}) custom-call(s32[1]{0:T(128)} %copy.25.live, s32[256]{0:T(256)S(1)} %copy-done, s32[256]{0:T(256)S(1)} %get-tuple-element.27.place, s32[256]{0:T(256)S(1)} %get-tuple-element.28.share, s32[256]{0:T(256)S(1)} %get-tuple-element.26.origin, f32[1024]{0:T(1024)S(1)} %fusion.3.factor, ...), custom_call_target="tpu_custom_call" | custom-call | flops 30000001024 | bytes 1048576 | tf_op jit(solution)/shard_map/pallas_call | solution.py:357
  103.2 0.9 all_to_all.34
  104.1 22.3 %all-to-all-start.2 = ((f32[32,36,128]{2,1,0:T(8,128)}), f32[32,36,128]{2,1,0:T(8,128)S(1)}, u32[]{:S(2)}, u32[]{:S(2)}) async-start(f32[32,36,128]{2,1,0:T(8,128)} %all_to_all.34), calls=%async_computation.2 | async-start | bytes 1310720 | tf_op jit(solution)/shard_map/all_to_all | solution.py:459
  126.5 8.1 %shard_map.99 = (f32[32,8,128]{2,1,0:T(8,128)S(1)}, f32[1152,128]{1,0:T(8,128)S(1)}) custom-call(s32[1]{0:T(128)} %copy.25.live, s32[256]{0:T(256)S(1)} %copy-done, s32[256]{0:T(256)S(1)} %get-tuple-element.27.place, s32[256]{0:T(256)S(1)} %get-tuple-element.28.share, s32[256]{0:T(256)S(1)} %get-tuple-element.26.origin, f32[1024]{0:T(1024)S(1)} %fusion.3.factor, ...), custom_call_target="tpu_custom_call" | custom-call | flops 30000001024 | bytes 1048576 | tf_op jit(solution)/shard_map/pallas_call | solution.py:357
  134.6 0.9 all_to_all.37
  135.5 10.1 %all-to-all-done.2 = f32[32,36,128]{2,1,0:T(8,128)S(1)} async-done(((f32[32,36,128]{2,1,0:T(8,128)}), f32[32,36,128]{2,1,0:T(8,128)S(1)}, u32[]{:S(2)}, u32[]{:S(2)}) %all-to-all-start.2) | async-done | bytes 589856 | tf_op jit(solution)/shard_map/all_to_all | solution.py:459
  145.6 14.7 %all-to-all-start.3 = ((f32[32,36,128]{2,1,0:T(8,128)}), f32[32,36,128]{2,1,0:T(8,128)S(1)}, u32[]{:S(2)}, u32[]{:S(2)}) async-start(f32[32,36,128]{2,1,0:T(8,128)} %all_to_all.37), calls=%async_computation.3 | async-start | bytes 1310720 | tf_op jit(solution)/shard_map/all_to_all | solution.py:459
  160.3 21.2 %shard_map.100.refs_1_ = f32[32,8,128]{2,1,0:T(8,128)S(1)} custom-call(f32[34]{0:T(128)S(1)} %dynamic_slice.3.factor, f32[2]{0:T(128)S(1)} %add_convert_fusion.1.ends, f32[34,8,128]{2,1,0:T(8,128)S(1)} %pad_maximum_fusion.state), custom_call_target="tpu_custom_call" | custom-call | flops 20000000000 | bytes 1048576 | tf_op jit(solution)/shard_map/pallas_call | solution.py:340
  181.6 4.4 %shard_map.101 = (f32[3,4096]{1,0:T(4,128)}, f32[3,4096]{1,0:T(4,128)}) custom-call(s32[384]{0:T(512)S(1)} %reshape.80.refs_0_, f32[32,8,128]{2,1,0:T(8,128)S(1)} %shard_map.100.refs_1_, f32[32,8,128]{2,1,0:T(8,128)S(1)} %get-tuple-element.15.refs_2_, f32[1152,128]{1,0:T(8,128)S(1)} %all_to_all.36.refs_3_, f32[1152,128]{1,0:T(8,128)S(1)} %all_to_all.39.refs_4_), custom_call_target="tpu_custom_call" | custom-call | tf_op jit(solution)/shard_map/pallas_call | solution.py:377
  (32 shorter events, 0.4 us)
Async XLA Ops:
  0.7 8.0 %copy-start.2 = (f32[3,4096]{1,0:T(4,128)S(1)}, f32[3,4096]{1,0:T(4,128)}, u32[]{:S(2)}) copy-start(f32[3,4096]{1,0:T(4,128)} %param.9) | copy-start | bytes 147460
  1.7 22.2 %collective-permute-start.1 = (f32[1,8,128]{2,1,0:T(8,128)S(1)}, f32[1,8,128]{2,1,0:T(8,128)S(1)}, u32[]{:S(2)}, u32[]{:S(2)}) collective-permute-start(f32[1,8,128]{2,1,0:T(8,128)S(1)} %get-tuple-element.21), channel_id=1, source_target_pairs={{1,0},{2,1},{3,2},{4,3},{5,4},{6,5},{7,6},{9,8},{10,9},{11,10},{12... | collective-permute-start | bytes 12296 | tf_op jit(solution)/shard_map/ppermute | solution.py:467
  3.0 5.5 %copy-start.3 = (s32[256,1]{0,1:T(1,128)S(1)}, s32[256,1]{0,1:T(1,128)}, u32[]{:S(2)}) copy-start(s32[256,1]{0,1:T(1,128)} %param.12) | copy-start | bytes 3076
  3.0 20.9 %collective-permute-start = (f32[1,8,128]{2,1,0:T(8,128)S(1)}, f32[1,8,128]{2,1,0:T(8,128)S(1)}, u32[]{:S(2)}, u32[]{:S(2)}) collective-permute-start(f32[1,8,128]{2,1,0:T(8,128)S(1)} %get-tuple-element.20), channel_id=1, source_target_pairs={{0,1},{1,2},{2,3},{3,4},{4,5},{5,6},{6,7},{8,9},{9,10},{10,11},{11... | collective-permute-start | bytes 12296 | tf_op jit(solution)/shard_map/ppermute | solution.py:465
  9.4 0.7 copy-start.4
  10.5 0.7 copy-start.6
  26.8 23.6 %all-to-all-start.1 = ((f32[32,36,128]{2,1,0:T(8,128)}), f32[32,36,128]{2,1,0:T(8,128)S(1)}, u32[]{:S(2)}, u32[]{:S(2)}) async-start(f32[32,36,128]{2,1,0:T(8,128)} %all_to_all.31), calls=%async_computation.1 | async-start | bytes 1310720 | tf_op jit(solution)/shard_map/all_to_all | solution.py:459
  31.3 0.7 copy-start.1
  32.7 0.7 copy-start.5
  50.4 53.7 %all-to-all-start = ((f32[32,36,128]{2,1,0:T(8,128)}), f32[32,36,128]{2,1,0:T(8,128)S(1)}, u32[]{:S(2)}, u32[]{:S(2)}) async-start(f32[32,36,128]{2,1,0:T(8,128)} %all_to_all.28), calls=%async_computation | async-start | bytes 1310720 | tf_op jit(solution)/shard_map/all_to_all | solution.py:459
  53.1 0.7 copy-start
  104.1 41.5 %all-to-all-start.2 = ((f32[32,36,128]{2,1,0:T(8,128)}), f32[32,36,128]{2,1,0:T(8,128)S(1)}, u32[]{:S(2)}, u32[]{:S(2)}) async-start(f32[32,36,128]{2,1,0:T(8,128)} %all_to_all.34), calls=%async_computation.2 | async-start | bytes 1310720 | tf_op jit(solution)/shard_map/all_to_all | solution.py:459
  145.6 35.9 %all-to-all-start.3 = ((f32[32,36,128]{2,1,0:T(8,128)}), f32[32,36,128]{2,1,0:T(8,128)S(1)}, u32[]{:S(2)}, u32[]{:S(2)}) async-start(f32[32,36,128]{2,1,0:T(8,128)} %all_to_all.37), calls=%async_computation.3 | async-start | bytes 1310720 | tf_op jit(solution)/shard_map/all_to_all | solution.py:459

commit v3 on v2

--- a/solution.py
+++ b/solution.py
@@ -131,10 +131,11 @@
     return to_t, combine(sums, own_s)
 
 
-def exchange_kernel(rows, out, landing, send, receive):
+def exchange_kernel(rows, state, out, edges, landing, sides, send, receive, side_send, side_get):
     n = rows.shape[0]
     n_blk = lax.axis_size("blk")
-    me = lax.axis_index("rotor") * n_blk + lax.axis_index("blk")
+    rotor, place = lax.axis_index("rotor"), lax.axis_index("blk")
+    me = rotor * n_blk + place
 
     def where(peer):
         return (peer // n_blk, lax.rem(peer, n_blk))
@@ -164,11 +165,24 @@
             device_id_type=pl.DeviceIdType.MESH,
         )
 
+    def side(i):
+        block, step = ((state.shape[0] - 1, 1), (0, n_blk - 1))[i]
+        return pltpu.make_async_remote_copy(
+            src_ref=state.at[block],
+            dst_ref=sides.at[i],
+            send_sem=side_send.at[i],
+            recv_sem=side_get.at[i],
+            device_id=(rotor, lax.rem(place + step, n_blk)),
+            device_id_type=pl.DeviceIdType.MESH,
+        )
+
     def start(d, carry):
         copy(d).start()
         return carry
 
     lax.fori_loop(1, n, start, 0)
+    side(0).start()
+    side(1).start()
     landing[me] = rows[me]
 
     def finish(d, carry):
@@ -176,7 +190,10 @@
         return carry
 
     lax.fori_loop(1, n, finish, 0)
+    side(0).wait()
+    side(1).wait()
     out[...] = landing[...]
+    edges[...] = sides[...]
 
 
 def gather_kernel(asked, state, out):
@@ -218,17 +235,19 @@
         v, o = held(k)
         return pair(sources[k], v, o, front[k], v, o, False)[0]
 
-    total[1] = chain(0)[1] * ends[0]
-
-    def both(k, carry):
-        itself = alone(k)
-        to_t, to_s = chain(k)
-        total[k] += itself + to_t
-        total[k + 1] = to_s
-        return carry
-
-    lax.fori_loop(1, blocks, both, 0)
-    total[blocks] += alone(blocks) + chain(blocks)[0] * ends[1]
+    total[...] = jnp.zeros_like(total)
+    group = math.gcd(blocks, 4)
+
+    def several(j, carry):
+        ks = [j * group + i + 1 for i in range(group)]
+        terms = [(alone(k), chain(k - 1)) for k in ks]
+        for k, (itself, (to_t, to_s)) in zip(ks, terms):
+            total[k - 1] += to_t * jnp.where(k == 1, 0.0, 1.0)
+            total[k] += itself + to_s * jnp.where(k == 1, ends[0], 1.0)
+        return carry
+
+    lax.fori_loop(0, blocks // group, several, 0)
+    total[blocks] += chain(blocks)[0] * ends[1]
     out[...] = total[1 : blocks + 1]
 
 
@@ -256,22 +275,15 @@
         vt, ot = values[t], tuple(own[t, i] for i in range(5))
         return t, p, pair(source_front(base), vs, os, front[t], vt, ot, True)
 
-    def add(t, p, terms):
-        acc[t] += terms[0]
-        back[pl.ds(p * 6, 6)] = jnp.concatenate([terms[1][:3], terms[1][4:7]], axis=0)
-
-    def step(i, carry):
-        add(*one(i))
-        return carry
-
-    def two(i, carry):
-        first_one, second_one = one(2 * i), one(2 * i + 1)
-        add(*first_one)
-        add(*second_one)
-        return carry
-
-    lax.fori_loop(0, count // 2, two, 0)
-    lax.fori_loop(count // 2 * 2, count, step, 0)
+    def step(j, carry):
+        at = [j * GROUP + i for i in range(GROUP)]
+        done = [one(jnp.minimum(i, count - 1)) for i in at]
+        for i, (t, p, (to_t, to_s)) in zip(at, done):
+            acc[t] += to_t * jnp.where(i < count, 1.0, 0.0)
+            back[pl.ds(p * 6, 6)] = jnp.concatenate([to_s[:3], to_s[4:7]], axis=0)
+        return carry
+
+    lax.fori_loop(0, (count + GROUP - 1) // GROUP, step, 0)
 
 
 def final_kernel(*refs):
@@ -309,20 +321,24 @@
 params = pltpu.CompilerParams(vmem_limit_bytes=24 * 2**20)
 
 
-def exchange(rows):
+def exchange(rows, state):
     n = rows.shape[0]
+    edges = jax.ShapeDtypeStruct((2,) + state.shape[1:], f32)
     return pl.pallas_call(
         exchange_kernel,
-        out_shape=jax.ShapeDtypeStruct(rows.shape, f32),
-        in_specs=[vmem],
-        out_specs=vmem,
+        out_shape=(jax.ShapeDtypeStruct(rows.shape, f32), edges),
+        in_specs=[vmem, vmem],
+        out_specs=(vmem, vmem),
         scratch_shapes=[
             pltpu.VMEM(rows.shape, f32),
+            pltpu.VMEM(edges.shape, f32),
             pltpu.SemaphoreType.DMA((n,)),
             pltpu.SemaphoreType.DMA((n,)),
+            pltpu.SemaphoreType.DMA((2,)),
+            pltpu.SemaphoreType.DMA((2,)),
         ],
         compiler_params=pltpu.CompilerParams(collective_id=0, has_side_effects=True),
-    )(rows)
+    )(rows, state)
 
 
 def gather(asked, state):
@@ -385,6 +401,7 @@
 
 
 PARTS = 2
+GROUP = 8
 
 
 def local(
@@ -438,7 +455,12 @@
     )
     used = PARTS * each
     rows = jnp.pad(rows, ((0, 0), (0, -rows.shape[1] % 128)))
-    got = exchange(rows[:, None, :])[:, 0]
+    state = jnp.concatenate(
+        [positions, strengths, jnp.zeros((2, positions.shape[1]), f32)], axis=0
+    )
+    state = state.reshape(ROWS, blocks, width).transpose(1, 0, 2)
+    got, edges = exchange(rows[:, None, :], state)
+    got = got[:, 0]
     asked = got[:, :used].astype(jnp.int32)
     asked = asked.reshape(devices, PARTS, each).transpose(1, 0, 2)
     member = (
@@ -450,25 +472,10 @@
     blade_factor = circulation / (totals / jnp.maximum(counted, 1.0) + 1e-06)
     factor = jnp.sum(member * blade_factor[None, :], axis=1)
 
-    state = jnp.concatenate(
-        [positions, strengths, jnp.zeros((2, positions.shape[1]), f32)], axis=0
-    )
-    state = state.reshape(ROWS, blocks, width).transpose(1, 0, 2)
-
     def swap(flat):
         return lax.all_to_all(flat, AXES, split_axis=0, concat_axis=0, tiled=True)
 
-    up = [(i, i + 1) for i in range(n_blk - 1)]
-    down = [(i + 1, i) for i in range(n_blk - 1)]
-    padded = jnp.concatenate(
-        [
-            lax.ppermute(state[blocks - 1 :], "blk", up),
-            state,
-            lax.ppermute(state[:1], "blk", down),
-        ],
-        axis=0,
-    )
-    state, padded = lax.optimization_barrier((state, padded))
+    padded = jnp.concatenate([edges[:1], state, edges[1:]], axis=0)
     arrived = [swap(gather(asked[i].reshape(-1), state)) for i in range(PARTS)]
     ends = jnp.stack([place > 0, place < n_blk - 1]).astype(f32)
     around = jnp.concatenate([jnp.zeros((1,), f32), factor, jnp.zeros((1,), f32)])
@@ -479,6 +486,8 @@
     returned = []
     for i in range(PARTS):
         acc, back = tiles(i, scalars, state, arrived[i], acc)
+        if returned:
+            back, returned[-1] = lax.optimization_barrier((back, returned[-1]))
         returned.append(swap(back))
     padded, acc = lax.optimization_barrier((padded, acc))
     near = near_field(near_factor, ends, padded)

time: 187 us -> 154 us (0.82)
  starting transfers between devices: 50.9 us -> 17.5 us
  waiting for transfers between devices: 24.1 us -> 16.2 us
  Pallas kernels: 97.7 us -> 104 us
    all_to_all x4, starting transfers between devices: 44.1 us -> 17.5 us  [swap(): return lax.all_to_all(flat, AXES, split_axis=0, concat_axis=0, tiled=True)]
    pallas_call x2, Pallas kernels: 57.6 us -> 67.7 us  [tiles(): pl.pallas_call(functools.partial(tile_kernel, part), out_shape=(jax.Shape...]
    all_to_all x4, waiting for transfers between devices: 24.1 us -> 16.2 us  [swap(): return lax.all_to_all(flat, AXES, split_axis=0, concat_axis=0, tiled=True)]
    ppermute x2 -> x0, starting transfers between devices: 6.76 us -> none  [the longest x1 5.47 us: local(): lax.ppermute(state[blocks - 1:], 'blk', up)]
    pallas_call x1, Pallas kernels: 21.2 us -> 16.3 us  [near_field(): pl.pallas_call(near_kernel, out_shape=jax.ShapeDtypeStruct((padded - 2, R...]
  transfers between devices with their start and end apart: 6 -> 4, of which waited for: 2 -> 2; matrix products, arithmetic and copies ran while one was open for 2% -> 1% of each run, Pallas kernels for 49% -> 57%
where the time goes in v3:
time: 154 us; the launch traced here: 151 us
  Pallas kernels  104 us (68%)
  starting transfers between devices  17.5 us (11%)
  waiting for transfers between devices  16.2 us (11%)
  local copies, waits for them, and re-layouts  9.21 us (6%)
  other arithmetic  3.28 us (2%)
  between operations  1.54 us (1%)
    pallas_call x2, Pallas kernels, tiles(): pl.pallas_call(functools.partial(tile_kernel, part), out_shape=(jax.Shape...  67.7 us
    all_to_all x4, starting transfers between devices, swap(): return lax.all_to_all(flat, AXES, split_axis=0, concat_axis=0, tiled=True)  17.5 us
    pallas_call x1, Pallas kernels, near_field(): pl.pallas_call(near_kernel, out_shape=jax.ShapeDtypeStruct((padded - 2, R...  16.3 us
    all_to_all x4, waiting for transfers between devices, swap(): return lax.all_to_all(flat, AXES, split_axis=0, concat_axis=0, tiled=True)  16.2 us
    pallas_call x1, Pallas kernels, exchange(): pl.pallas_call(exchange_kernel, out_shape=(jax.ShapeDtypeStruct(rows.shap...  11.7 us
    pallas_call x1, Pallas kernels, finish(): pl.pallas_call(final_kernel, out_shape=(shape, shape), in_specs=[smem] +...  4.37 us
    pallas_call x2, Pallas kernels, gather(): pl.pallas_call(gather_kernel, out_shape=jax.ShapeDtypeStruct((asked.shape...  3.73 us
    all_to_all x8, local copies, waits for them, and re-layouts, swap(): return lax.all_to_all(flat, AXES, split_axis=0, concat_axis=0, tiled=True)  3.71 us
  transfers between devices with their start and end apart: 4, of which 2 were waited for; matrix products, arithmetic and copies ran while one was open for 1% of the time, Pallas kernels for 57%

profile of v3, /device:TPU:0, one launch (start us, length us, event | category | flops | bytes accessed | tf_op | source)
XLA Modules:
  0.0 151.5 jit_solution(10482983108805606437)
XLA Ops:
  0.6 0.7 copy-done.5
  1.3 0.2 convert_reduce_fusion
  2.2 0.7 multiply_add_fusion
  2.9 0.3 select_reduce_fusion
  3.2 0.1 copy.19
  3.3 0.1 bitcast_reduce_fusion
  3.4 0.5 copy-done.8
  3.9 0.1 pad_maximum_fusion.2
  4.0 0.6 pad.4
  4.6 0.1 pad.12.clone
  4.7 0.7 maximum_bitcast_fusion.state
  5.4 11.7 %shard_map.95 = (f32[32,1,128]{2,1,0:T(1,128)}, f32[2,8,128]{2,1,0:T(8,128)}) custom-call(f32[32,1,128]{2,1,0:T(1,128)} %bitcast.21, f32[32,8,128]{2,1,0:T(8,128)} %maximum_bitcast_fusion.state), custom_call_target="tpu_custom_call" | custom-call | tf_op jit(solution)/shard_map/pallas_call | solution.py:327
  17.1 0.7 slice_convert_fusion
  17.8 0.1 copy.21
  17.9 0.1 copy.24
  18.0 0.1 reshape_squeeze.7.asked
  18.1 1.9 %shard_map.97 = f32[1152,128]{1,0:T(8,128)S(1)} custom-call(s32[192]{0:T(256)S(1)} %reshape_squeeze.7.asked, f32[32,8,128]{2,1,0:T(8,128)S(1)} %copy-done), custom_call_target="tpu_custom_call" | custom-call | tf_op jit(solution)/shard_map/pallas_call | solution.py:345
  20.0 0.9 all_to_all.32
  20.9 5.1 %all-to-all-start.1 = ((f32[32,36,128]{2,1,0:T(8,128)}), f32[32,36,128]{2,1,0:T(8,128)S(1)}, u32[]{:S(2)}, u32[]{:S(2)}) async-start(f32[32,36,128]{2,1,0:T(8,128)} %all_to_all.32), calls=%async_computation.1 | async-start | bytes 1310720 | tf_op jit(solution)/shard_map/all_to_all | solution.py:476
  26.0 0.1 copy.22
  26.1 0.6 copy-done.3
  26.7 0.1 fusion.6
  26.8 0.1 eq.76
  26.9 0.1 mul.44
  26.9 0.1 copy.23
  27.0 0.1 reshape_squeeze.6.asked
  27.1 1.9 %shard_map.96 = f32[1152,128]{1,0:T(8,128)S(1)} custom-call(s32[192]{0:T(256)S(1)} %reshape_squeeze.6.asked, f32[32,8,128]{2,1,0:T(8,128)S(1)} %copy-done), custom_call_target="tpu_custom_call" | custom-call | tf_op jit(solution)/shard_map/pallas_call | solution.py:345
  29.0 0.9 all_to_all.29
  29.9 0.1 reshape.81.refs_0_
  30.0 0.2 fusion.2
  30.2 0.7 copy-done.7
  30.9 0.1 fusion.3.factor
  31.0 0.1 concatenate.18
  31.1 0.1 dynamic_slice.3.factor
  31.2 0.1 add_convert_fusion.1.ends
  31.2 0.5 copy-done.6
  31.8 13.3 %all-to-all-done.1 = f32[32,36,128]{2,1,0:T(8,128)S(1)} async-done(((f32[32,36,128]{2,1,0:T(8,128)}), f32[32,36,128]{2,1,0:T(8,128)S(1)}, u32[]{:S(2)}, u32[]{:S(2)}) %all-to-all-start.1) | async-done | bytes 589856 | tf_op jit(solution)/shard_map/all_to_all | solution.py:476
  45.1 2.6 %all-to-all-start = ((f32[32,36,128]{2,1,0:T(8,128)}), f32[32,36,128]{2,1,0:T(8,128)S(1)}, u32[]{:S(2)}, u32[]{:S(2)}) async-start(f32[32,36,128]{2,1,0:T(8,128)} %all_to_all.29), calls=%async_computation | async-start | bytes 1310720 | tf_op jit(solution)/shard_map/all_to_all | solution.py:476
  47.8 0.7 copy-done.1
  48.5 45.3 %shard_map.98 = (f32[32,8,128]{2,1,0:T(8,128)S(1)}, f32[1152,128]{1,0:T(8,128)S(1)}) custom-call(s32[1]{0:T(128)} %copy.25.live, s32[256]{0:T(256)S(1)} %copy-done.1, s32[256]{0:T(256)S(1)} %get-tuple-element.31.place, s32[256]{0:T(256)S(1)} %get-tuple-element.32.share, s32[256]{0:T(256)S(1)} %get-tuple-element.30.origin, f32[1024]{0:T(1024)S(1)} %fusion.3.factor, ...), custom_call_target="tpu_custom_call" | custom-call | flops 30000001024 | bytes 1048576 | tf_op jit(solution)/shard_map/pallas_call | solution.py:373
  93.8 0.9 all_to_all.35
  94.7 6.8 %all-to-all-start.2 = ((f32[32,36,128]{2,1,0:T(8,128)}), f32[32,36,128]{2,1,0:T(8,128)S(1)}, u32[]{:S(2)}, u32[]{:S(2)}) async-start(f32[32,36,128]{2,1,0:T(8,128)} %all_to_all.35), calls=%async_computation.2 | async-start | bytes 1310720 | tf_op jit(solution)/shard_map/all_to_all | solution.py:476
  101.5 22.3 %shard_map.99 = (f32[32,8,128]{2,1,0:T(8,128)S(1)}, f32[1152,128]{1,0:T(8,128)S(1)}) custom-call(s32[1]{0:T(128)} %copy.25.live, s32[256]{0:T(256)S(1)} %copy-done.1, s32[256]{0:T(256)S(1)} %get-tuple-element.31.place, s32[256]{0:T(256)S(1)} %get-tuple-element.32.share, s32[256]{0:T(256)S(1)} %get-tuple-element.30.origin, f32[1024]{0:T(1024)S(1)} %fusion.3.factor, ...), custom_call_target="tpu_custom_call" | custom-call | flops 30000001024 | bytes 1048576 | tf_op jit(solution)/shard_map/pallas_call | solution.py:373
  123.9 0.9 all_to_all.38
  124.8 3.1 %all-to-all-start.3 = ((f32[32,36,128]{2,1,0:T(8,128)}), f32[32,36,128]{2,1,0:T(8,128)S(1)}, u32[]{:S(2)}, u32[]{:S(2)}) async-start(f32[32,36,128]{2,1,0:T(8,128)} %all_to_all.38), calls=%async_computation.3 | async-start | bytes 1310720 | tf_op jit(solution)/shard_map/all_to_all | solution.py:476
  127.9 16.3 %shard_map.100.refs_1_ = f32[32,8,128]{2,1,0:T(8,128)S(1)} custom-call(f32[34]{0:T(128)S(1)} %dynamic_slice.3.factor, f32[2]{0:T(128)S(1)} %add_convert_fusion.1.ends, f32[34,8,128]{2,1,0:T(8,128)S(1)} %pad_maximum_fusion.state), custom_call_target="tpu_custom_call" | custom-call | flops 20000000000 | bytes 1048576 | tf_op jit(solution)/shard_map/pallas_call | solution.py:356
  144.2 2.9 %all-to-all-done.3 = f32[32,36,128]{2,1,0:T(8,128)S(1)} async-done(((f32[32,36,128]{2,1,0:T(8,128)}), f32[32,36,128]{2,1,0:T(8,128)S(1)}, u32[]{:S(2)}, u32[]{:S(2)}) %all-to-all-start.3) | async-done | bytes 589856 | tf_op jit(solution)/shard_map/all_to_all | solution.py:476
  147.1 4.4 %shard_map.101 = (f32[3,4096]{1,0:T(4,128)}, f32[3,4096]{1,0:T(4,128)}) custom-call(s32[384]{0:T(512)S(1)} %reshape.81.refs_0_, f32[32,8,128]{2,1,0:T(8,128)S(1)} %shard_map.100.refs_1_, f32[32,8,128]{2,1,0:T(8,128)S(1)} %get-tuple-element.17.refs_2_, f32[1152,128]{1,0:T(8,128)S(1)} %all_to_all.37.refs_3_, f32[1152,128]{1,0:T(8,128)S(1)} %all_to_all.40.refs_4_), custom_call_target="tpu_custom_call" | custom-call | tf_op jit(solution)/shard_map/pallas_call | solution.py:393
  (32 shorter events, 0.3 us)
Async XLA Ops:
  0.6 0.7 copy-start.5
  0.6 2.6 %copy-start.2 = (f32[3,4096]{1,0:T(4,128)S(1)}, f32[3,4096]{1,0:T(4,128)}, u32[]{:S(2)}) copy-start(f32[3,4096]{1,0:T(4,128)} %param.9) | copy-start | bytes 147460
  3.3 0.7 copy-start.8
  3.3 1.4 copy-start.4
  5.4 12.7 %copy-start = (f32[32,8,128]{2,1,0:T(8,128)S(1)}, f32[32,8,128]{2,1,0:T(8,128)}, u32[]{:S(2)}) copy-start(f32[32,8,128]{2,1,0:T(8,128)} %maximum_bitcast_fusion.state) | copy-start | bytes 393220
  20.9 24.3 %all-to-all-start.1 = ((f32[32,36,128]{2,1,0:T(8,128)}), f32[32,36,128]{2,1,0:T(8,128)S(1)}, u32[]{:S(2)}, u32[]{:S(2)}) async-start(f32[32,36,128]{2,1,0:T(8,128)} %all_to_all.32), calls=%async_computation.1 | async-start | bytes 1310720 | tf_op jit(solution)/shard_map/all_to_all | solution.py:476
  26.0 0.7 copy-start.3
  30.2 0.7 copy-start.7
  31.1 0.7 copy-start.6
  45.1 49.6 %all-to-all-start = ((f32[32,36,128]{2,1,0:T(8,128)}), f32[32,36,128]{2,1,0:T(8,128)S(1)}, u32[]{:S(2)}, u32[]{:S(2)}) async-start(f32[32,36,128]{2,1,0:T(8,128)} %all_to_all.29), calls=%async_computation | async-start | bytes 1310720 | tf_op jit(solution)/shard_map/all_to_all | solution.py:476
  47.8 0.7 copy-start.1
  94.7 29.2 %all-to-all-start.2 = ((f32[32,36,128]{2,1,0:T(8,128)}), f32[32,36,128]{2,1,0:T(8,128)S(1)}, u32[]{:S(2)}, u32[]{:S(2)}) async-start(f32[32,36,128]{2,1,0:T(8,128)} %all_to_all.35), calls=%async_computation.2 | async-start | bytes 1310720 | tf_op jit(solution)/shard_map/all_to_all | solution.py:476
  124.8 22.2 %all-to-all-start.3 = ((f32[32,36,128]{2,1,0:T(8,128)}), f32[32,36,128]{2,1,0:T(8,128)S(1)}, u32[]{:S(2)}, u32[]{:S(2)}) async-start(f32[32,36,128]{2,1,0:T(8,128)} %all_to_all.38), calls=%async_computation.3 | async-start | bytes 1310720 | tf_op jit(solution)/shard_map/all_to_all | solution.py:476

commit v4 on v3

--- a/solution.py
+++ b/solution.py
@@ -291,11 +291,12 @@
     returned, (velocity, rate, total) = refs[3:-3], refs[-3:]
     blocks, _, width = near.shape
     total[pl.ds(0, blocks)] = near[...] + acc[...]
-    slots = asked.shape[0] // len(returned)
-    for i, got in enumerate(returned):
-
-        def step(p, carry):
-            index = asked[i * slots + p]
+    base = 0
+    for got in returned:
+        slots = got.shape[0] // 6
+
+        def step(p, carry, got=got, base=base):
+            index = asked[base + p]
             index = jnp.where(index < 0, blocks, index)
             terms = got[pl.ds(p * 6, 6)]
             gap = jnp.zeros((1, width), f32)
@@ -303,6 +304,7 @@
             return carry
 
         lax.fori_loop(0, slots, step, 0)
+        base += slots
     for k in range(blocks):
         velocity[:, k * width : (k + 1) * width] = total[k][:3]
         rate[:, k * width : (k + 1) * width] = total[k][4:7]
@@ -400,7 +402,6 @@
     )(asked, near, acc, *returned)
 
 
-PARTS = 2
 GROUP = 8
 
 
@@ -422,18 +423,23 @@
     me = lax.axis_index("rotor") * n_blk + place
     capacity = tile_target.shape[0]
     slot_count = max(2, (3 * capacity + 2 * devices - 1) // (2 * devices))
-    each = -(-slot_count // PARTS)
+    early = max(1, slot_count // 3)
+    bounds = ((0, early), (early, slot_count))
 
     source_dev = tile_source_dev[:, 0]
     ids = jnp.arange(capacity, dtype=jnp.int32)
     earlier = (source_dev[:, None] == source_dev[None, :]) & (ids[:, None] > ids[None, :])
     rank = jnp.sum(earlier.astype(jnp.int32), axis=1)
-    share = rank // each
-    spot = source_dev * each + rank % each
+    share = (rank >= early).astype(jnp.int32)
+    spot = jnp.where(
+        rank < early,
+        source_dev * early + rank,
+        source_dev * (slot_count - early) + rank - early,
+    )
     origin = source_dev * blocks + tile_source_blk
     ask = jnp.where(ids < tile_count[0], tile_source_blk, -1)
     peer_hot = source_dev[None, :] == jnp.arange(devices, dtype=jnp.int32)[:, None]
-    rank_hot = rank[None, :] == jnp.arange(PARTS * each, dtype=jnp.int32)[:, None]
+    rank_hot = rank[None, :] == jnp.arange(slot_count, dtype=jnp.int32)[:, None]
     request = (
         jnp.sum(
             jnp.where(
@@ -453,7 +459,7 @@
         ],
         axis=1,
     )
-    used = PARTS * each
+    used = slot_count
     rows = jnp.pad(rows, ((0, 0), (0, -rows.shape[1] % 128)))
     state = jnp.concatenate(
         [positions, strengths, jnp.zeros((2, positions.shape[1]), f32)], axis=0
@@ -462,7 +468,7 @@
     got, edges = exchange(rows[:, None, :], state)
     got = got[:, 0]
     asked = got[:, :used].astype(jnp.int32)
-    asked = asked.reshape(devices, PARTS, each).transpose(1, 0, 2)
+    asked = [asked[:, low:high].reshape(-1) for low, high in bounds]
     member = (
         got[:, used + blocks : used + 2 * blocks].reshape(-1, 1)
         == jnp.arange(circulation.shape[0], dtype=jnp.int32).astype(f32)[None, :]
@@ -476,7 +482,7 @@
         return lax.all_to_all(flat, AXES, split_axis=0, concat_axis=0, tiled=True)
 
     padded = jnp.concatenate([edges[:1], state, edges[1:]], axis=0)
-    arrived = [swap(gather(asked[i].reshape(-1), state)) for i in range(PARTS)]
+    arrived = [swap(gather(part, state)) for part in asked]
     ends = jnp.stack([place > 0, place < n_blk - 1]).astype(f32)
     around = jnp.concatenate([jnp.zeros((1,), f32), factor, jnp.zeros((1,), f32)])
     near_factor = lax.dynamic_slice_in_dim(around, me * blocks, blocks + 2)
@@ -484,14 +490,14 @@
     scalars = (tile_count, tile_target, spot, share, origin, factor, first)
     acc = jnp.zeros((blocks, ROWS, width), f32)
     returned = []
-    for i in range(PARTS):
+    for i in range(len(bounds)):
         acc, back = tiles(i, scalars, state, arrived[i], acc)
         if returned:
             back, returned[-1] = lax.optimization_barrier((back, returned[-1]))
         returned.append(swap(back))
     padded, acc = lax.optimization_barrier((padded, acc))
     near = near_field(near_factor, ends, padded)
-    return finish(asked.reshape(-1), near, acc, returned)
+    return finish(jnp.concatenate(asked), near, acc, returned)
 
 
 def solution(mesh):

time: 154 us -> 149 us (0.968); the launches traced: 151 us -> 149 us
  starting transfers between devices: 17.5 us -> 45.2 us
  Pallas kernels: 104 us -> 80.8 us
  local copies, waits for them, and re-layouts: 9.21 us -> 4.42 us
  waiting for transfers between devices: 16.2 us -> 13.8 us
    all_to_all x4, starting transfers between devices: 17.5 us -> 45.2 us  [swap(): return lax.all_to_all(flat, AXES, split_axis=0, concat_axis=0, tiled=True)]
    pallas_call x2, Pallas kernels: 67.7 us -> 43 us  [tiles(): pl.pallas_call(functools.partial(tile_kernel, part), out_shape=(jax.Shape...]
    all_to_all x8 -> x0, local copies, waits for them, and re-layouts: 3.71 us -> none  [swap(): return lax.all_to_all(flat, AXES, split_axis=0, concat_axis=0, tiled=True)]
    all_to_all x4, waiting for transfers between devices: 16.2 us -> 13.8 us  [swap(): return lax.all_to_all(flat, AXES, split_axis=0, concat_axis=0, tiled=True)]
    pallas_call x2, Pallas kernels: 3.73 us -> 5.35 us  [gather(): pl.pallas_call(gather_kernel, out_shape=jax.ShapeDtypeStruct((asked.shape...]
  transfers between devices with their start and end apart: 4 -> 4, of which waited for: 2 -> 2; matrix products, arithmetic and copies ran while one was open for 1% -> 1% of each run, Pallas kernels for 57% -> 42%
where the time goes in v4:
time: 149 us
  Pallas kernels  80.8 us (54%)
  starting transfers between devices  45.2 us (30%)
  waiting for transfers between devices  13.8 us (9%)
  local copies, waits for them, and re-layouts  4.42 us (3%)
  other arithmetic  3.28 us (2%)
    all_to_all x4, starting transfers between devices, swap(): return lax.all_to_all(flat, AXES, split_axis=0, concat_axis=0, tiled=True)  45.2 us
    pallas_call x2, Pallas kernels, tiles(): pl.pallas_call(functools.partial(tile_kernel, part), out_shape=(jax.Shape...  43 us
    pallas_call x1, Pallas kernels, near_field(): pl.pallas_call(near_kernel, out_shape=jax.ShapeDtypeStruct((padded - 2, R...  16.3 us
    all_to_all x4, waiting for transfers between devices, swap(): return lax.all_to_all(flat, AXES, split_axis=0, concat_axis=0, tiled=True)  13.8 us
    pallas_call x1, Pallas kernels, exchange(): pl.pallas_call(exchange_kernel, out_shape=(jax.ShapeDtypeStruct(rows.shap...  11.7 us
    pallas_call x2, Pallas kernels, gather(): pl.pallas_call(gather_kernel, out_shape=jax.ShapeDtypeStruct((asked.shape...  5.35 us
    pallas_call x1, Pallas kernels, finish(): pl.pallas_call(final_kernel, out_shape=(shape, shape), in_specs=[smem] +...  4.41 us
    unnamed x18, local copies, waits for them, and re-layouts  3 us
  transfers between devices with their start and end apart: 4, of which 2 were waited for; matrix products, arithmetic and copies ran while one was open for 1% of the time, Pallas kernels for 42%

profile of v4, /device:TPU:0, one launch (start us, length us, event | category | flops | bytes accessed | tf_op | source)
XLA Modules:
  0.0 148.9 jit_solution(13523257347951186082)
XLA Ops:
  0.6 0.0 copy-start.5
  0.6 0.0 copy-start.2
  0.6 0.7 copy-done.5
  1.3 0.2 convert_reduce_fusion
  2.2 0.7 multiply_add_fusion
  2.9 0.3 select_reduce_fusion
  3.1 0.1 copy.11
  3.2 0.0 copy-start.8
  3.3 0.0 copy-start.4
  3.3 0.1 bitcast_reduce_fusion
  3.4 0.5 copy-done.8
  3.9 0.1 pad_maximum_fusion.2
  4.0 0.6 pad.4
  4.6 0.1 pad.14.clone
  4.7 0.0 copy-done.4
  4.7 0.7 maximum_bitcast_fusion.state
  5.4 11.7 %shard_map.95 = (f32[32,1,128]{2,1,0:T(1,128)}, f32[2,8,128]{2,1,0:T(8,128)}) custom-call(f32[32,1,128]{2,1,0:T(1,128)} %bitcast.30, f32[32,8,128]{2,1,0:T(8,128)} %maximum_bitcast_fusion.state), custom_call_target="tpu_custom_call" | custom-call | tf_op jit(solution)/shard_map/pallas_call | solution.py:329
  17.1 0.7 slice_convert_fusion
  17.8 0.1 reshape.80.asked
  17.9 2.2 %shard_map.97 = f32[768,128]{1,0:T(8,128)} custom-call(s32[128]{0:T(128)S(1)} %reshape.80.asked, f32[32,8,128]{2,1,0:T(8,128)S(1)} %copy-done), custom_call_target="tpu_custom_call" | custom-call | tf_op jit(solution)/shard_map/pallas_call | solution.py:347
  20.1 5.1 %all-to-all-start.1 = ((f32[32,24,128]{2,1,0:T(8,128)}), f32[32,24,128]{2,1,0:T(8,128)S(1)}, u32[]{:S(2)}, u32[]{:S(2)}) async-start(f32[32,24,128]{2,1,0:T(8,128)} %bitcast.13), calls=%async_computation.1 | async-start | bytes 786432 | tf_op jit(solution)/shard_map/all_to_all | solution.py:482
  25.2 0.1 fusion.5
  25.3 0.1 slice.30
  25.4 0.1 eq.74
  25.4 0.1 mul.47
  25.5 0.2 fusion.2
  25.7 0.0 copy-start.7
  25.7 0.7 copy-done.7
  26.4 0.1 fusion.3.factor
  26.5 0.1 reshape.81.asked
  26.6 3.2 %shard_map.96 = f32[1536,128]{1,0:T(8,128)} custom-call(s32[256]{0:T(256)S(1)} %reshape.81.asked, f32[32,8,128]{2,1,0:T(8,128)S(1)} %copy-done), custom_call_target="tpu_custom_call" | custom-call | tf_op jit(solution)/shard_map/pallas_call | solution.py:347
  29.8 0.1 concatenate.22
  29.9 0.1 dynamic_slice.3.factor
  29.9 0.1 add_convert_fusion.1.ends
  30.0 0.5 copy-done.6
  30.6 8.2 %all-to-all-done.1 = f32[32,24,128]{2,1,0:T(8,128)S(1)} async-done(((f32[32,24,128]{2,1,0:T(8,128)}), f32[32,24,128]{2,1,0:T(8,128)S(1)}, u32[]{:S(2)}, u32[]{:S(2)}) %all-to-all-start.1) | async-done | bytes 393248 | tf_op jit(solution)/shard_map/all_to_all | solution.py:482
  38.7 2.6 %all-to-all-start = ((f32[32,48,128]{2,1,0:T(8,128)}), f32[32,48,128]{2,1,0:T(8,128)S(1)}, u32[]{:S(2)}, u32[]{:S(2)}) async-start(f32[32,48,128]{2,1,0:T(8,128)} %bitcast.11), calls=%async_computation | async-start | bytes 1572864 | tf_op jit(solution)/shard_map/all_to_all | solution.py:482
  41.4 0.0 copy-start.1
  41.4 0.7 copy-done.1
  42.1 28.1 %shard_map.98 = (f32[32,8,128]{2,1,0:T(8,128)S(1)}, f32[768,128]{1,0:T(8,128)}) custom-call(s32[1]{0:T(128)} %copy.13.live, s32[256]{0:T(256)S(1)} %copy-done.1, s32[256]{0:T(256)S(1)} %get-tuple-element.29.place, s32[256]{0:T(256)S(1)} %compare_convert_fusion.1.share, s32[256]{0:T(256)S(1)} %get-tuple-element.28.origin, f32[1024]{0:T(1024)S(1)} %fusion.3.factor, ...), custom_call_target="tpu_custom_call" | custom-call | flops 30000001024 | bytes 1048576 | tf_op jit(solution)/shard_map/pallas_call | solution.py:375
  70.2 0.0 all-to-all-done
  70.2 12.0 %all-to-all-start.2 = ((f32[32,24,128]{2,1,0:T(8,128)}), f32[32,24,128]{2,1,0:T(8,128)S(1)}, u32[]{:S(2)}, u32[]{:S(2)}) async-start(f32[32,24,128]{2,1,0:T(8,128)} %bitcast.15), calls=%async_computation.2 | async-start | bytes 786432 | tf_op jit(solution)/shard_map/all_to_all | solution.py:482
  82.2 14.9 %shard_map.99 = (f32[32,8,128]{2,1,0:T(8,128)S(1)}, f32[1536,128]{1,0:T(8,128)}) custom-call(s32[1]{0:T(128)} %copy.13.live, s32[256]{0:T(256)S(1)} %copy-done.1, s32[256]{0:T(256)S(1)} %get-tuple-element.29.place, s32[256]{0:T(256)S(1)} %compare_convert_fusion.1.share, s32[256]{0:T(256)S(1)} %get-tuple-element.28.origin, f32[1024]{0:T(1024)S(1)} %fusion.3.factor, ...), custom_call_target="tpu_custom_call" | custom-call | flops 30000001024 | bytes 1048576 | tf_op jit(solution)/shard_map/pallas_call | solution.py:375
  97.1 0.0 all-to-all-done.2
  97.1 25.4 %all-to-all-start.3 = ((f32[32,48,128]{2,1,0:T(8,128)}), f32[32,48,128]{2,1,0:T(8,128)S(1)}, u32[]{:S(2)}, u32[]{:S(2)}) async-start(f32[32,48,128]{2,1,0:T(8,128)} %bitcast.17), calls=%async_computation.3 | async-start | bytes 1572864 | tf_op jit(solution)/shard_map/all_to_all | solution.py:482
  122.6 16.3 %shard_map.100.refs_1_ = f32[32,8,128]{2,1,0:T(8,128)S(1)} custom-call(f32[34]{0:T(128)S(1)} %dynamic_slice.3.factor, f32[2]{0:T(128)S(1)} %add_convert_fusion.1.ends, f32[34,8,128]{2,1,0:T(8,128)S(1)} %pad_maximum_fusion.state), custom_call_target="tpu_custom_call" | custom-call | flops 20000000000 | bytes 1048576 | tf_op jit(solution)/shard_map/pallas_call | solution.py:358
  138.9 5.7 %all-to-all-done.3 = f32[32,48,128]{2,1,0:T(8,128)S(1)} async-done(((f32[32,48,128]{2,1,0:T(8,128)}), f32[32,48,128]{2,1,0:T(8,128)S(1)}, u32[]{:S(2)}, u32[]{:S(2)}) %all-to-all-start.3) | async-done | bytes 786464 | tf_op jit(solution)/shard_map/all_to_all | solution.py:482
  144.5 4.4 %shard_map.101 = (f32[3,4096]{1,0:T(4,128)}, f32[3,4096]{1,0:T(4,128)}) custom-call(s32[384]{0:T(512)S(1)} %pad_add_fusion.refs_0_, f32[32,8,128]{2,1,0:T(8,128)S(1)} %shard_map.100.refs_1_, f32[32,8,128]{2,1,0:T(8,128)S(1)} %get-tuple-element.17.refs_2_, f32[768,128]{1,0:T(8,128)S(1)} %bitcast.24, f32[1536,128]{1,0:T(8,128)S(1)} %bitcast.23), custom_call_target="tpu_custom_call" | custom-call | tf_op jit(solution)/shard_map/pallas_call | solution.py:395
  (20 shorter events, 0.1 us)
Async XLA Ops:
  0.6 0.7 copy-start.5
  0.6 2.6 %copy-start.2 = (f32[3,4096]{1,0:T(4,128)S(1)}, f32[3,4096]{1,0:T(4,128)}, u32[]{:S(2)}) copy-start(f32[3,4096]{1,0:T(4,128)} %param.9) | copy-start | bytes 147460
  3.2 0.7 copy-start.8
  3.3 1.4 copy-start.4
  5.4 12.5 %copy-start = (f32[32,8,128]{2,1,0:T(8,128)S(1)}, f32[32,8,128]{2,1,0:T(8,128)}, u32[]{:S(2)}) copy-start(f32[32,8,128]{2,1,0:T(8,128)} %maximum_bitcast_fusion.state) | copy-start | bytes 393220
  20.1 5.1 %copy-start.3 = (f32[32,1,128]{2,1,0:T(1,128)S(1)}, f32[32,1,128]{2,1,0:T(1,128)}, u32[]{:S(2)}) copy-start(f32[32,1,128]{2,1,0:T(1,128)} %get-tuple-element.12) | copy-start | bytes 49156
  20.1 18.7 %all-to-all-start.1 = ((f32[32,24,128]{2,1,0:T(8,128)}), f32[32,24,128]{2,1,0:T(8,128)S(1)}, u32[]{:S(2)}, u32[]{:S(2)}) async-start(f32[32,24,128]{2,1,0:T(8,128)} %bitcast.13), calls=%async_computation.1 | async-start | bytes 786432 | tf_op jit(solution)/shard_map/all_to_all | solution.py:482
  25.7 0.7 copy-start.7
  29.9 0.7 copy-start.6
  38.7 31.5 %all-to-all-start = ((f32[32,48,128]{2,1,0:T(8,128)}), f32[32,48,128]{2,1,0:T(8,128)S(1)}, u32[]{:S(2)}, u32[]{:S(2)}) async-start(f32[32,48,128]{2,1,0:T(8,128)} %bitcast.11), calls=%async_computation | async-start | bytes 1572864 | tf_op jit(solution)/shard_map/all_to_all | solution.py:482
  41.4 0.7 copy-start.1
  70.2 26.9 %all-to-all-start.2 = ((f32[32,24,128]{2,1,0:T(8,128)}), f32[32,24,128]{2,1,0:T(8,128)S(1)}, u32[]{:S(2)}, u32[]{:S(2)}) async-start(f32[32,24,128]{2,1,0:T(8,128)} %bitcast.15), calls=%async_computation.2 | async-start | bytes 786432 | tf_op jit(solution)/shard_map/all_to_all | solution.py:482
  97.1 47.4 %all-to-all-start.3 = ((f32[32,48,128]{2,1,0:T(8,128)}), f32[32,48,128]{2,1,0:T(8,128)S(1)}, u32[]{:S(2)}, u32[]{:S(2)}) async-start(f32[32,48,128]{2,1,0:T(8,128)} %bitcast.17), calls=%async_computation.3 | async-start | bytes 1572864 | tf_op jit(solution)/shard_map/all_to_all | solution.py:482
